TPU v7x, 512 devices: a whole 4x4x16 slice. The times are simulated.
512 devices in a mesh: inp: 64 (over z, y), tblk: 8 (over x, core).
Axes of the slice: x: 4, y: 4, z: 16, core: 2. Of those that a mesh axis runs over, the one named last changes fastest.
Arguments:
- samples: bfloat16 [1024, 192, 2048], P('inp', 'tblk'), may hold values from -40 to 40
- kept: int32 [384], replicated, may hold values from 0 to 1023, as said below
Outputs:
- visibilities: bfloat16 [384, 2, 1024, 1024], P('inp', None, 'tblk')
Inputs may be any that keep to these rules, and one draw needn't show every extreme that they name: `kept`: 384 distinct channel indices in increasing order; 0 and 1023 are always among them.
All inputs are finite; a program needn't handle non-finite values.
Results may differ from a plain program's by a relative error of at most 0.0042.
Values may be sent and summed in bfloat16 or wider, within the bound.
No kernel may reach another device: no remote copies, remote signals or barrier semaphores. Data moves between devices by JAX's collectives and lax.ppermute only.
A program may use at most 64 MiB of HBM per device.

v0:
```python
import math

import jax
import jax.numpy as jnp
from jax import lax
from jax.sharding import PartitionSpec as P

TAPS = 4


def from_behind(block, axis, distance):
    devices = range(lax.axis_size(axis))
    route = [(i - distance, i) for i in devices if i - distance in devices]
    return lax.ppermute(block, axis, route)


def window_table(taps, length_total):
    span = taps * length_total
    m = jnp.arange(span, dtype=jnp.float32)
    proto = jnp.sinc((m - span / 2.0) / length_total) * (
        0.5 - 0.5 * jnp.cos(2.0 * math.pi * m / span)
    )
    return proto.reshape(taps, length_total)[::-1]


def fourier_table(kept, length_total):
    current_position = jnp.arange(length_total, dtype=jnp.int32)
    phase = kept[:, None] * current_position[None, :] % length_total
    angle = phase.astype(jnp.float32) * (2.0 * math.pi / length_total)
    return jnp.stack([jnp.cos(angle), -jnp.sin(angle)], axis=1).astype(jnp.bfloat16)


def correlate(picked, column_list):
    real_part = picked[:, 0]
    imag_part = picked[:, 1]
    first = jnp.stack([real_part, imag_part], axis=1)
    second = jnp.stack([imag_part, -real_part], axis=1)
    left_part = jnp.stack([first, second], axis=1)
    return jnp.einsum(
        "xydhq,xdaq->xyha", left_part, column_list, preferred_element_type=jnp.float32
    )


def local(samples, kept):
    width_in, spd, length_total = samples.shape
    sample_history = from_behind(samples[:, spd - (TAPS - 1) :, :], "tblk", 1)
    extended_samples = jnp.concatenate([sample_history, samples], axis=1)
    weights = window_table(TAPS, length_total)
    filtered = jnp.zeros((width_in, spd, length_total), jnp.float32)
    for tap in range(TAPS):
        first = TAPS - 1 - tap
        filtered = filtered + weights[tap] * extended_samples[:, first : first + spd, :].astype(
            jnp.float32
        )
    filtered = filtered.astype(jnp.bfloat16)
    table = fourier_table(kept, length_total)
    spectra = jnp.einsum("cpn,isn->cpis", table, filtered, preferred_element_type=jnp.float32)
    spectra = (spectra / math.sqrt(length_total)).astype(jnp.bfloat16)
    count = lax.axis_size("tblk")
    block = lax.axis_index("tblk")
    whole_time = lax.all_gather(spectra, "tblk", axis=3, tiled=True)
    owned = lax.all_to_all(whole_time, "inp", split_axis=0, concat_axis=2, tiled=True)
    rows = owned.shape[2] // count
    picked = lax.dynamic_slice_in_dim(owned, block * rows, rows, 2)
    totals = correlate(picked, owned)
    return (totals / (spd * count)).astype(jnp.bfloat16)


def solution(mesh):
    placed = (P("inp", "tblk", None), P())
    return jax.shard_map(
        local, mesh=mesh, in_specs=placed, out_specs=P("inp", None, "tblk", None), check_vma=False
    )
```

profile of v0, /device:TPU:8, one launch (start us, length us, event | category | flops | bytes accessed | tf_op | source)
XLA Modules:
  0.0 400.9 jit_solution(4398140830763226787)
XLA Ops:
  6.5 0.0 copy-start.1
  6.5 0.0 all-gather.2.cloned.1.call-start
  6.5 1.3 slice.37
  7.9 1.8 collective-permute-start
  9.6 0.3 fusion.27
  9.9 14.3 %cosine_convert_fusion = (bf16[384,1,2048]{2,0,1:T(8,128)(2,1)S(1)}, bf16[384,1,2048]{2,0,1:T(8,128)(2,1)S(1)}) fusion(s32[384]{0:T(512)} %param.3), kind=kLoop, calls=%fused_computation.14 | loop fusion | flops 13369344 | bytes 3147264 | tf_op jit(solution)/shard_map/convert
  24.2 0.0 collective-permute-done
  24.3 0.0 copy-done.1
  24.3 4.0 fusion.16
  28.2 0.0 all-gather.2.cloned.1.call-update
  28.3 47.6 %all-gather.2.cloned.1.call-done = bf16[384,2,16,192]{0,3,2,1:T(8,128)(2,1)} async-done(((bf16[384,2,16,24]{0,3,2,1:T(8,128)(2,1)}), bf16[384,2,16,192]{0,3,2,1:T(8,128)(2,1)}) %all-gather.2.cloned.1.call-update) | async-done | bytes 4718608 | tf_op jit(solution)/shard_map/all_gather | solution.py:61
  75.9 9.0 %copy.9 = bf16[384,2,16,192]{3,2,1,0:T(8,128)(2,1)} copy(bf16[384,2,16,192]{0,3,2,1:T(8,128)(2,1)} %all-gather.2.cloned.1.call-done) | data formatting | bytes 9437184 | tf_op jit(solution)/shard_map/all_gather | solution.py:61
  84.9 15.9 %all-to-all-start = ((bf16[384,2,16,192]{3,2,1,0:T(8,128)(2,1)}), bf16[384,2,16,192]{3,2,1,0:T(8,128)(2,1)}, u32[]{:S(2)}, u32[]{:S(2)}) async-start(bf16[384,2,16,192]{3,2,1,0:T(8,128)(2,1)} %copy.9), calls=%async_computation | async-start | bytes 12582912 | tf_op jit(solution)/shard_map/all_to_all | solution.py:62
  100.8 280.3 %all-to-all-done = bf16[384,2,16,192]{3,2,1,0:T(8,128)(2,1)} async-done(((bf16[384,2,16,192]{3,2,1,0:T(8,128)(2,1)}), bf16[384,2,16,192]{3,2,1,0:T(8,128)(2,1)}, u32[]{:S(2)}, u32[]{:S(2)}) %all-to-all-start) | async-done | bytes 4718624 | tf_op jit(solution)/shard_map/all_to_all | solution.py:62
  381.1 3.4 copy.10
  384.5 0.0 copy-start
  384.5 2.7 copy-done
  387.2 0.1 constant_dynamic-slice_fusion
  387.2 0.3 copy.18
  387.6 0.1 fusion.35
  387.7 0.1 maximum_bitcast_fusion.6
  387.7 6.4 %fusion = bf16[6,2,128,1024]{3,2,1,0:T(8,128)(2,1)} fusion(bf16[6,2,1024,192,1]{3,2,1,4,0:T(8,128)(2,1)} %bitcast.38, bf16[6,1,2,128,192]{3,4,2,1,0:T(8,128)(2,1)S(1)} %maximum_bitcast_fusion.6, bf16[6,1,2,128,192]{3,4,2,1,0:T(8,128)(2,1)S(1)} %bitcast.39), kind=kOutput, calls=%fused_computation.1 | convolution fusion | flops 1211695104 | bytes 9043968 | tf_op jit(solution)/shard_map/xydhq,xdaq->xyha/dot_general | solution.py:39
  (1 shorter events, 0.0 us)
Async XLA Ops:
  6.5 17.7 %copy-start.1 = (bf16[16,24,2048]{2,1,0:T(8,128)(2,1)S(1)}, bf16[16,24,2048]{2,1,0:T(8,128)(2,1)}, u32[]{:S(2)}) copy-start(bf16[16,24,2048]{2,1,0:T(8,128)(2,1)} %param.2) | copy-start | bytes 4718596
  6.5 69.3 %all-gather.2.cloned.1.call-start = ((), (), s32[]{:S(2)}) async-start(), calls=%async_computation.1 | async-start | bytes 5308416 | tf_op jit(solution)/shard_map/all_gather | solution.py:61
  7.9 16.4 %collective-permute-start = (bf16[16,3,2048]{2,1,0:T(4,128)(2,1)S(1)}, bf16[16,3,2048]{2,1,0:T(4,128)(2,1)S(1)}, u32[]{:S(2)}, u32[]{:S(2)}) collective-permute-start(bf16[16,3,2048]{2,1,0:T(4,128)(2,1)S(1)} %slice.37), channel_id=1, source_target_pairs={{0,1},{1,2},{2,3},{3,4},{4,5},{5,6},{6,7},{8,9},{9,10},{10,11},{11... | collective-permute-start | bytes 589832 | tf_op jit(solution)/shard_map/ppermute | solution.py:14
  84.9 296.2 %all-to-all-start = ((bf16[384,2,16,192]{3,2,1,0:T(8,128)(2,1)}), bf16[384,2,16,192]{3,2,1,0:T(8,128)(2,1)}, u32[]{:S(2)}, u32[]{:S(2)}) async-start(bf16[384,2,16,192]{3,2,1,0:T(8,128)(2,1)} %copy.9), calls=%async_computation | async-start | bytes 12582912 | tf_op jit(solution)/shard_map/all_to_all | solution.py:62
  384.5 2.7 copy-start
Sparse Core Ops, SparseCore 0:
  28.4 47.4 all-gather.1
where the time goes:
time: 401 us
  waiting for transfers between devices  328 us (82%)
  starting transfers between devices  17.7 us (4%)
  local copies, waits for them, and re-layouts  16.9 us (4%)
  other arithmetic  14.7 us (4%)
  between operations  13.5 us (3%)
  matrix products  10.3 us (3%)
    all_to_all x1, waiting for transfers between devices, local(): lax.all_to_all(whole_time, 'inp', split_axis=0, concat_axis=2, tiled=True)  280 us
    all_gather x1, waiting for transfers between devices, local(): whole_time = lax.all_gather(spectra, 'tblk', axis=3, tiled=True)  47.6 us
    all_to_all x1, starting transfers between devices, local(): lax.all_to_all(whole_time, 'inp', split_axis=0, concat_axis=2, tiled=True)  15.9 us
    another operation x1, other arithmetic  14.3 us
    all_gather x1, local copies, waits for them, and re-layouts, local(): whole_time = lax.all_gather(spectra, 'tblk', axis=3, tiled=True)  9.04 us
  transfers between devices with their start and end apart: 3, of which 2 were waited for; matrix products, arithmetic and copies ran while one was open for 4% of the time, Pallas kernels for 0%

commit v1 on v0

v1 whole, which is shorter than its diff:
```python
import math

import jax
import jax.numpy as jnp
from jax import lax
from jax.sharding import PartitionSpec as P

TAPS = 4


def from_behind(block, axis, distance):
    devices = range(lax.axis_size(axis))
    route = [(i - distance, i) for i in devices if i - distance in devices]
    return lax.ppermute(block, axis, route)


def window_table(taps, length_total):
    span = taps * length_total
    m = jnp.arange(span, dtype=jnp.float32)
    proto = jnp.sinc((m - span / 2.0) / length_total) * (
        0.5 - 0.5 * jnp.cos(2.0 * math.pi * m / span)
    )
    return proto.reshape(taps, length_total)[::-1]


def fourier_table(kept, length_total):
    lo = jnp.arange(128, dtype=jnp.int32)
    hi = jnp.arange(length_total // 128, dtype=jnp.int32) * 128
    step = 2.0 * math.pi / length_total
    a = (kept[:, None] * hi[None, :] % length_total).astype(jnp.float32) * step
    b = (kept[:, None] * lo[None, :] % length_total).astype(jnp.float32) * step
    ca, sa = jnp.cos(a)[:, :, None], jnp.sin(a)[:, :, None]
    cb, sb = jnp.cos(b)[:, None, :], jnp.sin(b)[:, None, :]
    re = (ca * cb - sa * sb).reshape(-1, length_total)
    im = -(sa * cb + ca * sb).reshape(-1, length_total)
    return jnp.stack([re, im], axis=1).astype(jnp.bfloat16)


def local(samples, kept):
    width_in, spd, length_total = samples.shape
    keep = kept.shape[0]
    groups = lax.axis_size("inp")
    count = lax.axis_size("tblk")
    block = lax.axis_index("tblk")
    sample_history = from_behind(samples[:, spd - (TAPS - 1) :, :], "tblk", 1)
    extended_samples = jnp.concatenate([sample_history, samples], axis=1)
    weights = window_table(TAPS, length_total)
    filtered = jnp.zeros((width_in, spd, length_total), jnp.float32)
    for tap in range(TAPS):
        first = TAPS - 1 - tap
        filtered = filtered + weights[tap] * extended_samples[:, first : first + spd, :].astype(
            jnp.float32
        )
    filtered = filtered.astype(jnp.bfloat16).reshape(width_in * spd, length_total)
    table = fourier_table(kept, length_total).reshape(2 * keep, length_total)
    spectra = jnp.einsum("kn,rn->kr", table, filtered, preferred_element_type=jnp.float32)
    spectra = (spectra / math.sqrt(length_total)).astype(jnp.bfloat16)
    own = keep // groups
    spectra = spectra.reshape(groups, own * 2, width_in * spd)
    owned = lax.all_to_all(spectra, "inp", split_axis=0, concat_axis=0, tiled=True)
    owned = owned.reshape(groups, own, 2, width_in, spd).transpose(1, 2, 4, 0, 3)
    owned = owned.reshape(own, 2 * spd, groups * width_in)
    whole = lax.all_gather(owned, "tblk", axis=0)
    whole = whole.reshape(count, own, 2, spd, groups * width_in)
    rows = groups * width_in // count
    picked = lax.dynamic_slice_in_dim(whole, block * rows, rows, 4)
    first = picked
    second = jnp.stack([picked[:, :, 1], -picked[:, :, 0]], axis=2)
    left = jnp.stack([first, second], axis=2)
    totals = jnp.einsum("tcypsh,tcpsa->cyha", left, whole, preferred_element_type=jnp.float32)
    return (totals / (spd * count)).astype(jnp.bfloat16)


def solution(mesh):
    placed = (P("inp", "tblk", None), P())
    return jax.shard_map(
        local, mesh=mesh, in_specs=placed, out_specs=P("inp", None, "tblk", None), check_vma=False
    )
```

time: 401 us -> 160 us (0.40)
  the two profiles are of different devices: /device:TPU:8 before, /device:TPU:1 now
where the time goes in v1:
time: 160 us; the launch traced here: 159 us
  blocking collectives  61.7 us (39%)
  waiting for transfers between devices  34.3 us (21%)
  local copies, waits for them, and re-layouts  27.4 us (17%)
  between operations  13.5 us (8%)
  other arithmetic  9.42 us (6%)
  matrix products  8.51 us (5%)
  starting transfers between devices  4.51 us (3%)
    all_to_all x1, blocking collectives, local(): lax.all_to_all(spectra, 'inp', split_axis=0, concat_axis=0, tiled=True)  61.7 us
    all_gather x1, waiting for transfers between devices, local(): whole = lax.all_gather(owned, 'tblk', axis=0)  34.3 us
    another operation x2, local copies, waits for them, and re-layouts, local(): whole = lax.all_gather(owned, 'tblk', axis=0)  12.9 us
    dot_general x1, matrix products, local(): jnp.einsum('tcypsh,tcpsa->cyha', left, whole, preferred_element_type=jnp....  5.88 us
    another operation x1, local copies, waits for them, and re-layouts, fourier_table(): return jnp.stack([re, im], axis=1).astype(jnp.bfloat16)  5.78 us
    convert_element_type x1, other arithmetic, local(): filtered.astype(jnp.bfloat16).reshape(width_in * spd, length_total)  5.15 us
    ppermute x1, starting transfers between devices, from_behind(): return lax.ppermute(block, axis, route)  4.51 us
    convert_element_type x1, local copies, waits for them, and re-layouts, fourier_table(): return jnp.stack([re, im], axis=1).astype(jnp.bfloat16)  4.02 us
  transfers between devices with their start and end apart: 2, of which 1 were waited for; matrix products, arithmetic and copies ran while one was open for 9% of the time, Pallas kernels for 0%

profile of v1, /device:TPU:1, one launch (start us, length us, event | category | flops | bytes accessed | tf_op | source)
XLA Modules:
  0.0 159.4 jit_solution(13669549572481724793)
XLA Ops:
  6.5 0.0 all-gather.2.cloned.1.call-start
  6.5 1.2 slice.36
  7.7 4.5 %collective-permute-start = (bf16[16,3,2048]{2,1,0:T(4,128)(2,1)S(1)}, bf16[16,3,2048]{2,1,0:T(4,128)(2,1)}, u32[]{:S(2)}, u32[]{:S(2)}) collective-permute-start(bf16[16,3,2048]{2,1,0:T(4,128)(2,1)S(1)} %slice.36), channel_id=1, source_target_pairs={{0,1},{1,2},{2,3},{3,4},{4,5},{5,6},{6,7},{8,9},{9,10},{10,11},{11... | collective-permute-start | bytes 589832 | tf_op jit(solution)/shard_map/ppermute | solution.py:14
  12.3 0.3 fusion.24
  12.6 1.5 fusion.18
  14.1 0.9 fusion.34
  15.0 1.1 subtract_convert_fusion
  16.1 0.4 pad_maximum_fusion
  16.5 5.8 %copy.15 = bf16[384,2,2048]{2,1,0:T(2,128)(2,1)} copy(bf16[384,2,2048]{0,2,1:T(8,128)(2,1)S(1)} %pad_maximum_fusion) | data formatting | bytes 6291456 | tf_op jit(solution)/shard_map/stack | solution.py:36
  22.2 4.0 %convert_element_type.59 = bf16[768,2048]{1,0:T(8,128)(2,1)S(1)} reshape(bf16[384,2,2048]{2,1,0:T(2,128)(2,1)} %copy.15) | data formatting | bytes 6291456 | tf_op jit(solution)/shard_map/convert_element_type | solution.py:36
  26.3 0.0 collective-permute-done
  26.3 5.2 %add_convert_fusion = bf16[16,24,2048]{2,1,0:T(8,128)(2,1)S(1)} fusion(bf16[16,24,2048]{2,1,0:T(8,128)(2,1)} %param.2, bf16[16,3,2048]{2,1,0:T(4,128)(2,1)} %collective-permute-done, f32[2048]{0:T(1024)S(1)} %bitcast.34, f32[2048]{0:T(1024)S(1)} %bitcast.35, f32[2048]{0:T(1024)S(1)} %bitcast.36, f32[2048]{0:T(1024)S(1)} %bitcast.33), kind=kLoop, calls=%fused_computation.5 | loop fusion | flops 16515072 | bytes 3375104 | tf_op jit(solution)/shard_map/convert_element_type | solution.py:54
  31.4 2.6 %fusion.7 = bf16[768,384]{1,0:T(8,128)(2,1)} fusion(bf16[768,2048]{1,0:T(8,128)(2,1)S(1)} %convert_element_type.59, bf16[384,2048]{1,0:T(8,128)(2,1)S(1)} %bitcast.30), kind=kOutput, calls=%fused_computation.16 | convolution fusion | flops 1208549376 | bytes 5308416 | tf_op jit(solution)/shard_map/kn,rn->kr/dot_general | solution.py:56
  34.1 1.2 reshape.243
  35.3 61.7 %all_to_all.5 = bf16[64,12,384]{2,1,0:T(8,128)(2,1)S(1)} all-to-all(bf16[64,12,384]{2,1,0:T(8,128)(2,1)S(1)} %reshape.243), channel_id=1, replica_groups=mesh['inp'=64,'tblk'=8] {'inp'}, dimensions={0} | all-to-all | bytes 1179648 | tf_op jit(solution)/shard_map/all_to_all | solution.py:60
  97.0 1.0 copy.16
  98.1 3.4 %copy.23 = bf16[6,2,24,64,16]{4,3,2,1,0:T(8,128)(2,1)} copy(bf16[6,2,24,64,16]{3,2,4,1,0:T(8,128)(2,1)S(1)} %bitcast.29) | data formatting | bytes 1179648 | tf_op jit(solution)/shard_map/all_gather;reshape | solution.py:63
  101.5 9.5 %reshape.248 = bf16[1,6,48,1024]{3,2,1,0:T(8,128)(2,1)} reshape(bf16[6,2,24,64,16]{4,3,2,1,0:T(8,128)(2,1)} %copy.23) | data formatting | bytes 1179648 | tf_op jit(solution)/shard_map/all_gather;reshape | solution.py:63
  111.0 0.0 all-gather.2.cloned.1.call-update
  111.0 34.3 %all-gather.2.cloned.1.call-done = bf16[8,6,48,1024]{3,2,1,0:T(8,128)(2,1)} async-done(((bf16[1,6,48,1024]{3,2,1,0:T(8,128)(2,1)}), bf16[8,6,48,1024]{3,2,1,0:T(8,128)(2,1)}) %all-gather.2.cloned.1.call-update) | async-done | bytes 4718608 | tf_op jit(solution)/shard_map/all_gather | solution.py:63
  145.3 1.2 copy_bitcast_fusion
  146.5 0.1 fusion.36
  146.6 0.1 maximum_bitcast_fusion
  146.7 5.9 %fusion = bf16[6,2,128,1024]{3,2,1,0:T(8,128)(2,1)} fusion(bf16[8,6,2,24,1024,1]{4,3,2,1,0,5:T(8,128)(2,1)} %bitcast.32, bf16[8,6,1,2,24,128]{5,4,0,3,2,1:T(8,128)(2,1)S(1)} %maximum_bitcast_fusion, bf16[8,6,1,2,24,128]{5,4,0,3,2,1:T(8,128)(2,1)S(1)} %get-tuple-element.5), kind=kOutput, calls=%fused_computation.1 | convolution fusion | flops 1211695104 | bytes 9043968 | tf_op jit(solution)/shard_map/tcypsh,tcpsa->cyha/dot_general | solution.py:70
  (2 shorter events, 0.0 us)
Async XLA Ops:
  6.5 138.8 %all-gather.2.cloned.1.call-start = ((), (), s32[]{:S(2)}) async-start(), calls=%async_computation.1 | async-start | bytes 5308416 | tf_op jit(solution)/shard_map/all_gather | solution.py:63
  7.7 18.5 %collective-permute-start = (bf16[16,3,2048]{2,1,0:T(4,128)(2,1)S(1)}, bf16[16,3,2048]{2,1,0:T(4,128)(2,1)}, u32[]{:S(2)}, u32[]{:S(2)}) collective-permute-start(bf16[16,3,2048]{2,1,0:T(4,128)(2,1)S(1)} %slice.36), channel_id=1, source_target_pairs={{0,1},{1,2},{2,3},{3,4},{4,5},{5,6},{6,7},{8,9},{9,10},{10,11},{11... | collective-permute-start | bytes 589832 | tf_op jit(solution)/shard_map/ppermute | solution.py:14
Sparse Core Ops, SparseCore 0:
  111.1 34.1 all-gather.1

commit v2 on v0

v2 whole, which is shorter than its diff:
```python
import math

import jax
import jax.numpy as jnp
from jax import lax
from jax.experimental import pallas as pl
from jax.experimental.pallas import tpu as pltpu
from jax.sharding import PartitionSpec as P

TAPS = 4
L = 2048
G = 64
C = 6
Q = 12
I = 16
S = 24
F32, BF16 = jnp.float32, jnp.bfloat16
PARAMS = pltpu.CompilerParams(vmem_limit_bytes=40 * 1024 * 1024)
VMEM = pl.BlockSpec(memory_space=pltpu.VMEM)


def dot(a, b, ca, cb):
    return lax.dot_general(a, b, (((ca,), (cb,)), ((), ())), preferred_element_type=F32)


def iota(shape, dim):
    return lax.broadcasted_iota(jnp.int32, shape, dim)


def window_table(taps, length_total):
    span = taps * length_total
    m = jnp.arange(span, dtype=F32)
    proto = jnp.sinc((m - span / 2.0) / length_total) * (
        0.5 - 0.5 * jnp.cos(2.0 * math.pi * m / span)
    )
    return proto.reshape(taps, length_total)[::-1]


def cosine(m):
    r = jnp.abs(((m + L // 2) & (L - 1)) - L // 2)
    flip = r > L // 4
    r = jnp.where(flip, L // 2 - r, r)
    u = r.astype(F32) * (2.0 * math.pi / L)
    u = u * u
    acc = jnp.full_like(u, 1.0 / math.factorial(14) * -1.0)
    for k in range(6, -1, -1):
        acc = acc * u + (-1.0) ** k / math.factorial(2 * k)
    return jnp.where(flip, -acc, acc)


def table_kernel(kept_ref, table_ref, swap_ref):
    rows = G * Q
    half = G * 8
    r = iota((rows, 1), 0)
    low = r - half
    flat_a = (r // 8) * Q + r % 8
    flat_b = ((low // 4) % 2 * (G // 2) + low // 8) * Q + 8 + low % 4
    flat = jnp.where(r < half, flat_a, flat_b)
    keep = kept_ref.shape[1]
    hit = iota((rows, keep), 1) == flat // 2
    chan = jnp.sum(jnp.where(hit, kept_ref[...].astype(F32), 0.0), axis=1, keepdims=True)
    chan = chan.astype(jnp.int32)
    lane = iota((rows, 128), 1)
    a = chan * lane * 128 + (flat % 2) * (L // 4)
    b = chan * lane
    ca, sa = cosine(a), cosine(a + 3 * (L // 4))
    cb, sb = cosine(b), cosine(b + 3 * (L // 4))
    for h in range(L // 128):
        part = ca[:, h : h + 1] * cb - sa[:, h : h + 1] * sb
        table_ref[:, h * 128 : (h + 1) * 128] = part.astype(BF16)
    n = 1024
    for h in range(n // 128):
        col = iota((n, 128), 1)
        want = (col // 16) * 128 + h * 16 + col % 16
        swap_ref[:, h * 128 : (h + 1) * 128] = jnp.where(iota((n, 128), 0) == want, 1.0, 0.0).astype(BF16)


def spectra_kernel(table_ref, samples_ref, halo_ref, weights_ref, out_ref, filtered):
    step = 512
    row = iota((8, step), 0)

    def fir(pair, carry):
        for n in range(0, L, step):
            cols = slice(n, n + step)
            parts = []
            for one in range(2):
                i = pair * 2 + one
                now = samples_ref[i, :, cols].astype(F32)
                back = halo_ref[i, :, cols].astype(F32)
                back = jnp.concatenate([back, back], axis=0)
                total = weights_ref[0:1, cols] * now
                for d in range(1, TAPS):
                    moved = pltpu.roll(now, d, 0)
                    head = jnp.where(row < d, pltpu.roll(back, d, 0), moved[0:8])
                    moved = jnp.concatenate([head, moved[8:]], axis=0)
                    total = total + weights_ref[d : d + 1, cols] * moved
                parts.append(total)
            both = jnp.concatenate(parts, axis=0).astype(BF16)
            filtered[pl.ds(pl.multiple_of(pair * 2 * S, 2 * S), 2 * S), cols] = both
        return carry

    lax.fori_loop(0, I // 2, fir, 0)
    width = I * S
    col = iota((width, width), 1)
    order = jnp.where(iota((width, width), 0) == (col % I) * S + col // I, 1.0, 0.0).astype(BF16)
    scale = 1.0 / math.sqrt(L)

    def transform(first):
        value = dot(table_ref[first : first + 256, :], filtered[...], 1, 1) * scale
        value = dot(value.astype(BF16), order, 1, 0)
        return value.reshape(32, 8, width)

    rest = transform(512)
    turned = pltpu.roll(rest, 4, 1)
    top = iota((32, 8, 128), 1) < 4
    for a in range(2):
        main = transform(a * 256)
        here, there = (rest, turned) if a == 0 else (turned, rest)
        owners = slice(a * 32, (a + 1) * 32)
        out_ref[owners, 0:16, :] = jnp.concatenate(
            [main[:, :, 0:128], main[:, :, 128:256]], axis=1
        ).astype(BF16)
        mixed = jnp.where(top, here[:, :, 0:128], there[:, :, 128:256])
        out_ref[owners, 16:32, :] = jnp.concatenate([main[:, :, 256:384], mixed], axis=1).astype(BF16)
        out_ref[owners, 32:36, :] = here[:, 0:4, 256:384].astype(BF16)


def regroup_kernel(owned_ref, swap_ref, out_ref, rows_ref, wide_ref):
    units = 36
    for g in range(G):
        big, small = g // 8, g % 8
        rows_ref[big * 48 : big * 48 + units, small * 128 : (small + 1) * 128] = owned_ref[g]
    for s in range(8):
        wide_ref[s * 40 + 32 : s * 40 + 40, :] = jnp.zeros((8, 1024), F32)
    for h in range(4):
        cols = slice(h * 256, (h + 1) * 256)
        part = dot(rows_ref[...], swap_ref[:, cols], 1, 0)
        for big in range(8):
            for s in range(2):
                place = (h * 2 + s) * 40
                wide_ref[place : place + units, big * 128 : (big + 1) * 128] = part[
                    big * 48 : big * 48 + units, s * 128 : (s + 1) * 128
                ]
    shape = (Q * S, 320)
    r = iota(shape, 0)
    q, s = r // S, r % S
    third = s // 8
    unit = jnp.where(q < 8, third * 8 + q, 24 + third * 4 + q - 8)
    order = jnp.where(iota(shape, 1) == (s % 8) * 40 + unit, 1.0, 0.0).astype(BF16)
    out_ref[...] = dot(order, wide_ref[...].astype(BF16), 1, 0).astype(BF16)


def correlate_kernel(block_ref, *refs):
    blocks, out_ref = refs[:-1], refs[-1]
    c = pl.program_id(0)
    early = c < C // 2
    first = pl.multiple_of(block_ref[0] * 128, 128)
    right, left = [], []
    for half in range(2):
        own, up, down, far_a, far_b = blocks[half * 5 : half * 5 + 5]
        for ref in (own, up, down):
            right.append(ref[...])
            left.append(ref[:, pl.ds(first, 128)].astype(F32))
        right.append(jnp.where(early, far_a[...], far_b[...]))
        left.append(
            jnp.where(early, far_a[:, pl.ds(first, 128)].astype(F32), far_b[:, pl.ds(first, 128)].astype(F32))
        )
    right = jnp.concatenate(right, axis=0)
    other = [jnp.concatenate([v[S:], -v[:S]], axis=0) for v in left]
    left = jnp.concatenate([jnp.concatenate(left, axis=0), jnp.concatenate(other, axis=0)], axis=1)
    total = dot(left.astype(BF16), right, 0, 0) * (1.0 / (8 * S))
    out_ref[0] = total.reshape(2, 128, 1024).astype(BF16)


def local(samples, kept):
    block = lax.axis_index("tblk")
    steps = lax.axis_size("tblk")
    halo = lax.ppermute(samples[:, S - 4 :, :], "tblk", [(i, i + 1) for i in range(steps - 1)])
    weights = window_table(TAPS, L)
    table, swap = pl.pallas_call(
        table_kernel,
        out_shape=[
            jax.ShapeDtypeStruct((G * Q, L), BF16),
            jax.ShapeDtypeStruct((1024, 1024), BF16),
        ],
        in_specs=[VMEM],
        out_specs=[VMEM, VMEM],
        compiler_params=PARAMS,
        cost_estimate=pl.CostEstimate(flops=10_000_000, bytes_accessed=5_000_000, transcendentals=0),
    )(kept.reshape(1, -1))
    chunks = pl.pallas_call(
        spectra_kernel,
        out_shape=jax.ShapeDtypeStruct((G, 36, 128), BF16),
        in_specs=[VMEM] * 4,
        out_specs=VMEM,
        scratch_shapes=[pltpu.VMEM((I * S, L), BF16)],
        compiler_params=PARAMS,
    )(table, samples, halo, weights)
    owned = lax.all_to_all(chunks, "inp", split_axis=0, concat_axis=0, tiled=True)
    mine = pl.pallas_call(
        regroup_kernel,
        out_shape=jax.ShapeDtypeStruct((Q * S, 1024), BF16),
        in_specs=[VMEM] * 2,
        out_specs=VMEM,
        scratch_shapes=[pltpu.VMEM((384, 1024), BF16), pltpu.VMEM((320, 1024), F32)],
        compiler_params=PARAMS,
    )(owned, swap)
    core = [(i, i ^ 1) for i in range(steps)]
    plus = [(i, (i + 2) % steps) for i in range(steps)]
    minus = [(i, (i - 2) % steps) for i in range(steps)]
    send = lambda v, route: lax.ppermute(v, "tblk", route)
    up, down = send(mine, plus), send(mine, minus)
    mine_o = send(mine, core)
    mid = Q * S // 2
    far_a, far_b = send(up[:mid], plus), send(down[mid:], minus)
    up_o, down_o = send(up, core), send(down, core)
    far_ao, far_bo = send(far_a, core), send(far_b, core)
    near = pl.BlockSpec((2 * S, 1024), lambda c, b: (c, 0))
    head = pl.BlockSpec((2 * S, 1024), lambda c, b: (jnp.minimum(c, 2), 0))
    tail = pl.BlockSpec((2 * S, 1024), lambda c, b: (jnp.maximum(c - 3, 0), 0))
    specs = [near, near, near, head, tail] * 2
    return pl.pallas_call(
        correlate_kernel,
        out_shape=jax.ShapeDtypeStruct((C, 2, 128, 1024), BF16),
        grid_spec=pltpu.PrefetchScalarGridSpec(
            num_scalar_prefetch=1,
            grid=(C,),
            in_specs=specs,
            out_specs=pl.BlockSpec((1, 2, 128, 1024), lambda c, b: (c, 0, 0, 0)),
        ),
        compiler_params=PARAMS,
    )(block.reshape(1), mine, up, down, far_a, far_b, mine_o, up_o, down_o, far_ao, far_bo)


def solution(mesh):
    placed = (P("inp", "tblk", None), P())
    return jax.shard_map(
        local, mesh=mesh, in_specs=placed, out_specs=P("inp", None, "tblk", None), check_vma=False
    )
```

time: 401 us -> 119 us (0.30)
  the two profiles are of different devices: /device:TPU:8 before, /device:TPU:1 now
where the time goes in v2:
time: 119 us
  blocking collectives  56.4 us (47%)
  starting transfers between devices  28.9 us (24%)
  Pallas kernels  17.6 us (15%)
  waiting for transfers between devices  11.4 us (10%)
  local copies, waits for them, and re-layouts  3.73 us (3%)
    all_to_all x1, blocking collectives, local(): lax.all_to_all(chunks, 'inp', split_axis=0, concat_axis=0, tiled=True)  56.4 us
    ppermute x9, starting transfers between devices, local(): send = lambda v, route: lax.ppermute(v, 'tblk', route)  24.3 us
    ppermute x9, waiting for transfers between devices, local(): send = lambda v, route: lax.ppermute(v, 'tblk', route)  11.4 us
    pallas_call x1, Pallas kernels, local(): pl.pallas_call(correlate_kernel, out_shape=jax.ShapeDtypeStruct((C, 2, 12...  6.15 us
    pallas_call x1, Pallas kernels, local(): pl.pallas_call(table_kernel, out_shape=[jax.ShapeDtypeStruct((G * Q, L),...  5.69 us
    ppermute x1, starting transfers between devices, local(): lax.ppermute(samples[:, S - 4:, :], 'tblk', [(i, i + 1) for i in range(st...  4.51 us
    pallas_call x1, Pallas kernels, local(): pl.pallas_call(spectra_kernel, out_shape=jax.ShapeDtypeStruct((G, 36, 128...  4.31 us
  transfers between devices with their start and end apart: 10, of which 3 were waited for; matrix products, arithmetic and copies ran while one was open for 1% of the time, Pallas kernels for 5%

profile of v2, /device:TPU:1, one launch (start us, length us, event | category | flops | bytes accessed | tf_op | source)
XLA Modules:
  0.0 118.6 jit_solution(10588317223258296583)
XLA Ops:
  0.0 1.2 %slice.9 = bf16[16,4,2048]{2,1,0:T(4,128)(2,1)S(1)} slice(bf16[16,24,2048]{2,1,0:T(8,128)(2,1)} %samples_ref.1), slice={[0:16], [20:24], [0:2048]} | slice | bytes 524288 | tf_op jit(solution)/shard_map/slice | solution.py:178
  1.2 4.5 %collective-permute-start = (bf16[16,4,2048]{2,1,0:T(4,128)(2,1)S(1)}, bf16[16,4,2048]{2,1,0:T(4,128)(2,1)S(1)}, u32[]{:S(2)}, u32[]{:S(2)}) collective-permute-start(bf16[16,4,2048]{2,1,0:T(4,128)(2,1)S(1)} %slice.9), channel_id=1, source_target_pairs={{0,1},{1,2},{2,3},{3,4},{4,5},{5,6},{6,7},{8,9},{9,10},{10,11},{11... | collective-permute-start | bytes 786440 | tf_op jit(solution)/shard_map/ppermute | solution.py:178
  5.7 0.7 reshape.10.kept_ref
  6.4 0.3 fusion.5
  6.7 0.4 rev.3.weights_ref
  7.2 5.7 %shard_map.28 = (bf16[768,2048]{1,0:T(8,128)(2,1)S(1)}, bf16[1024,1024]{1,0:T(8,128)(2,1)S(1)}) custom-call(s32[1,384]{1,0:T(1,128)S(1)} %reshape.10.kept_ref), custom_call_target="tpu_custom_call" | custom-call | flops 10000000 | bytes 5000000 | tf_op jit(solution)/shard_map/pallas_call | solution.py:180
  12.9 0.0 collective-permute-done.halo_ref
  12.9 0.0 copy-start
  12.9 1.4 %copy-done = bf16[16,24,2048]{2,1,0:T(8,128)(2,1)S(1)} copy-done((bf16[16,24,2048]{2,1,0:T(8,128)(2,1)S(1)}, bf16[16,24,2048]{2,1,0:T(8,128)(2,1)}, u32[]{:S(2)}) %copy-start) | copy-done | bytes 1572888
  14.3 4.3 %shard_map.29 = bf16[64,36,128]{2,1,0:T(8,128)(2,1)S(1)} custom-call(bf16[768,2048]{1,0:T(8,128)(2,1)S(1)} %get-tuple-element.7.table_ref, bf16[16,24,2048]{2,1,0:T(8,128)(2,1)S(1)} %copy-done, bf16[16,4,2048]{2,1,0:T(4,128)(2,1)S(1)} %collective-permute-done.halo_ref, f32[4,2048]{1,0:T(4,128)S(1)} %rev.3.weights_ref), custom_call_target="tpu_custom_call" | custom-call | tf_op jit(solution)/shard_map/pallas_call | solution.py:191
  18.6 56.4 %all_to_all.5.owned_ref = bf16[64,36,128]{2,1,0:T(8,128)(2,1)S(1)} all-to-all(bf16[64,36,128]{2,1,0:T(8,128)(2,1)S(1)} %shard_map.29), channel_id=1, replica_groups=mesh['inp'=64,'tblk'=8] {'inp'}, dimensions={0} | all-to-all | bytes 1179648 | tf_op jit(solution)/shard_map/all_to_all | solution.py:199
  75.0 1.5 %shard_map.30.refs_0_ = bf16[288,1024]{1,0:T(8,128)(2,1)S(1)} custom-call(bf16[64,36,128]{2,1,0:T(8,128)(2,1)S(1)} %all_to_all.5.owned_ref, bf16[1024,1024]{1,0:T(8,128)(2,1)S(1)} %get-tuple-element.8.swap_ref), custom_call_target="tpu_custom_call" | custom-call | tf_op jit(solution)/shard_map/pallas_call | solution.py:200
  76.5 1.9 %collective-permute-start.2 = (bf16[288,1024]{1,0:T(8,128)(2,1)S(1)}, bf16[288,1024]{1,0:T(8,128)(2,1)S(1)}, u32[]{:S(2)}, u32[]{:S(2)}) collective-permute-start(bf16[288,1024]{1,0:T(8,128)(2,1)S(1)} %shard_map.30.refs_0_), channel_id=1, source_target_pairs={{0,6},{1,7},{2,0},{3,1},{4,2},{5,3},{6,4},{7,5},{8,14},{9,15},{10,... | collective-permute-start | bytes 1769480 | tf_op jit(solution)/shard_map/ppermute | solution.py:211
  78.4 3.4 %collective-permute-start.1 = (bf16[288,1024]{1,0:T(8,128)(2,1)S(1)}, bf16[288,1024]{1,0:T(8,128)(2,1)S(1)}, u32[]{:S(2)}, u32[]{:S(2)}) collective-permute-start(bf16[288,1024]{1,0:T(8,128)(2,1)S(1)} %shard_map.30.refs_0_), channel_id=1, source_target_pairs={{0,2},{1,3},{2,4},{3,5},{4,6},{5,7},{6,0},{7,1},{8,10},{9,11},{10,... | collective-permute-start | bytes 1769480 | tf_op jit(solution)/shard_map/ppermute | solution.py:211
  81.8 2.1 %collective-permute-start.5 = (bf16[288,1024]{1,0:T(8,128)(2,1)S(1)}, bf16[288,1024]{1,0:T(8,128)(2,1)S(1)}, u32[]{:S(2)}, u32[]{:S(2)}) collective-permute-start(bf16[288,1024]{1,0:T(8,128)(2,1)S(1)} %shard_map.30.refs_0_), channel_id=1, source_target_pairs={{0,1},{1,0},{2,3},{3,2},{4,5},{5,4},{6,7},{7,6},{8,9},{9,8},{10,11... | collective-permute-start | bytes 1769480 | tf_op jit(solution)/shard_map/ppermute | solution.py:211
  83.9 9.7 %collective-permute-done.2.refs_2_ = bf16[288,1024]{1,0:T(8,128)(2,1)S(1)} collective-permute-done((bf16[288,1024]{1,0:T(8,128)(2,1)S(1)}, bf16[288,1024]{1,0:T(8,128)(2,1)S(1)}, u32[]{:S(2)}, u32[]{:S(2)}) %collective-permute-start.2) | collective-permute-done | bytes 589856 | tf_op jit(solution)/shard_map/ppermute | solution.py:211
  93.6 2.4 %collective-permute-start.4 = (bf16[144,1024]{1,0:T(8,128)(2,1)S(1)}, bf16[144,1024]{1,0:T(8,128)(2,1)}, u32[]{:S(2)}, u32[]{:S(2)}) collective-permute-start(bf16[144,1024]{1,0:T(8,128)(2,1)S(1)} %slice.13), channel_id=1, source_target_pairs={{0,6},{1,7},{2,0},{3,1},{4,2},{5,3},{6,4},{7,5},{8,14},{9,15},{10,... | collective-permute-start | bytes 884744 | tf_op jit(solution)/shard_map/ppermute | solution.py:211
  96.1 0.3 collective-permute-done.1.refs_1_
  96.4 2.6 %collective-permute-start.3 = (bf16[144,1024]{1,0:T(8,128)(2,1)S(1)}, bf16[144,1024]{1,0:T(8,128)(2,1)}, u32[]{:S(2)}, u32[]{:S(2)}) collective-permute-start(bf16[144,1024]{1,0:T(8,128)(2,1)S(1)} %slice.12), channel_id=1, source_target_pairs={{0,2},{1,3},{2,4},{3,5},{4,6},{5,7},{6,0},{7,1},{8,10},{9,11},{10,... | collective-permute-start | bytes 884744 | tf_op jit(solution)/shard_map/ppermute | solution.py:211
  99.0 3.0 %collective-permute-start.7 = (bf16[288,1024]{1,0:T(8,128)(2,1)S(1)}, bf16[288,1024]{1,0:T(8,128)(2,1)S(1)}, u32[]{:S(2)}, u32[]{:S(2)}) collective-permute-start(bf16[288,1024]{1,0:T(8,128)(2,1)S(1)} %collective-permute-done.2.refs_2_), channel_id=1, source_target_pairs={{0,1},{1,0},{2,3},{3,2},{4,5},{5,4},{6,7},{7,6},{8,9},{9,8},{10,11... | collective-permute-start | bytes 1769480 | tf_op jit(solution)/shard_map/ppermute | solution.py:211
  102.0 1.9 %collective-permute-start.6 = (bf16[288,1024]{1,0:T(8,128)(2,1)S(1)}, bf16[288,1024]{1,0:T(8,128)(2,1)S(1)}, u32[]{:S(2)}, u32[]{:S(2)}) collective-permute-start(bf16[288,1024]{1,0:T(8,128)(2,1)S(1)} %collective-permute-done.1.refs_1_), channel_id=1, source_target_pairs={{0,1},{1,0},{2,3},{3,2},{4,5},{5,4},{6,7},{7,6},{8,9},{9,8},{10,11... | collective-permute-start | bytes 1769480 | tf_op jit(solution)/shard_map/ppermute | solution.py:211
  103.9 0.0 collective-permute-done.4.refs_4_
  103.9 3.0 %collective-permute-start.9 = (bf16[144,1024]{1,0:T(8,128)(2,1)}, bf16[144,1024]{1,0:T(8,128)(2,1)}, u32[]{:S(2)}, u32[]{:S(2)}) collective-permute-start(bf16[144,1024]{1,0:T(8,128)(2,1)} %collective-permute-done.4.refs_4_), channel_id=1, source_target_pairs={{0,1},{1,0},{2,3},{3,2},{4,5},{5,4},{6,7},{7,6},{8,9},{9,8},{10,11... | collective-permute-start | bytes 884744 | tf_op jit(solution)/shard_map/ppermute | solution.py:211
  107.0 0.0 collective-permute-done.3.refs_3_
  107.0 3.9 %collective-permute-start.8 = (bf16[144,1024]{1,0:T(8,128)(2,1)}, bf16[144,1024]{1,0:T(8,128)(2,1)}, u32[]{:S(2)}, u32[]{:S(2)}) collective-permute-start(bf16[144,1024]{1,0:T(8,128)(2,1)} %collective-permute-done.3.refs_3_), channel_id=1, source_target_pairs={{0,1},{1,0},{2,3},{3,2},{4,5},{5,4},{6,7},{7,6},{8,9},{9,8},{10,11... | collective-permute-start | bytes 884744 | tf_op jit(solution)/shard_map/ppermute | solution.py:211
  110.9 0.0 collective-permute-done.5.refs_5_
  110.9 0.0 collective-permute-done.9.refs_9_
  110.9 0.0 collective-permute-done.7.refs_7_
  110.9 1.5 %collective-permute-done.8.refs_8_ = bf16[144,1024]{1,0:T(8,128)(2,1)} collective-permute-done((bf16[144,1024]{1,0:T(8,128)(2,1)}, bf16[144,1024]{1,0:T(8,128)(2,1)}, u32[]{:S(2)}, u32[]{:S(2)}) %collective-permute-start.8) | collective-permute-done | bytes 294944 | tf_op jit(solution)/shard_map/ppermute | solution.py:211
  112.4 0.0 collective-permute-done.6.refs_6_
  112.4 6.2 %shard_map.31 = bf16[6,2,128,1024]{3,2,1,0:T(8,128)(2,1)} custom-call(s32[1]{0:T(128)} %bitcast.block_ref, bf16[288,1024]{1,0:T(8,128)(2,1)S(1)} %shard_map.30.refs_0_, bf16[288,1024]{1,0:T(8,128)(2,1)S(1)} %collective-permute-done.1.refs_1_, bf16[288,1024]{1,0:T(8,128)(2,1)S(1)} %collective-permute-done.2.refs_2_, ...), custom_call_target="tpu_custom_call" | custom-call | tf_op jit(solution)/shard_map/pallas_call | solution.py:222
  (2 shorter events, 0.0 us)
Async XLA Ops:
  1.2 11.7 %collective-permute-start = (bf16[16,4,2048]{2,1,0:T(4,128)(2,1)S(1)}, bf16[16,4,2048]{2,1,0:T(4,128)(2,1)S(1)}, u32[]{:S(2)}, u32[]{:S(2)}) collective-permute-start(bf16[16,4,2048]{2,1,0:T(4,128)(2,1)S(1)} %slice.9), channel_id=1, source_target_pairs={{0,1},{1,2},{2,3},{3,4},{4,5},{5,6},{6,7},{8,9},{9,10},{10,11},{11... | collective-permute-start | bytes 786440 | tf_op jit(solution)/shard_map/ppermute | solution.py:178
  12.9 1.4 %copy-start = (bf16[16,24,2048]{2,1,0:T(8,128)(2,1)S(1)}, bf16[16,24,2048]{2,1,0:T(8,128)(2,1)}, u32[]{:S(2)}) copy-start(bf16[16,24,2048]{2,1,0:T(8,128)(2,1)} %samples_ref.1) | copy-start | bytes 4718596
  76.5 17.1 %collective-permute-start.2 = (bf16[288,1024]{1,0:T(8,128)(2,1)S(1)}, bf16[288,1024]{1,0:T(8,128)(2,1)S(1)}, u32[]{:S(2)}, u32[]{:S(2)}) collective-permute-start(bf16[288,1024]{1,0:T(8,128)(2,1)S(1)} %shard_map.30.refs_0_), channel_id=1, source_target_pairs={{0,6},{1,7},{2,0},{3,1},{4,2},{5,3},{6,4},{7,5},{8,14},{9,15},{10,... | collective-permute-start | bytes 1769480 | tf_op jit(solution)/shard_map/ppermute | solution.py:211
  78.4 17.9 %collective-permute-start.1 = (bf16[288,1024]{1,0:T(8,128)(2,1)S(1)}, bf16[288,1024]{1,0:T(8,128)(2,1)S(1)}, u32[]{:S(2)}, u32[]{:S(2)}) collective-permute-start(bf16[288,1024]{1,0:T(8,128)(2,1)S(1)} %shard_map.30.refs_0_), channel_id=1, source_target_pairs={{0,2},{1,3},{2,4},{3,5},{4,6},{5,7},{6,0},{7,1},{8,10},{9,11},{10,... | collective-permute-start | bytes 1769480 | tf_op jit(solution)/shard_map/ppermute | solution.py:211
  81.8 29.1 %collective-permute-start.5 = (bf16[288,1024]{1,0:T(8,128)(2,1)S(1)}, bf16[288,1024]{1,0:T(8,128)(2,1)S(1)}, u32[]{:S(2)}, u32[]{:S(2)}) collective-permute-start(bf16[288,1024]{1,0:T(8,128)(2,1)S(1)} %shard_map.30.refs_0_), channel_id=1, source_target_pairs={{0,1},{1,0},{2,3},{3,2},{4,5},{5,4},{6,7},{7,6},{8,9},{9,8},{10,11... | collective-permute-start | bytes 1769480 | tf_op jit(solution)/shard_map/ppermute | solution.py:211
  93.6 10.3 %collective-permute-start.4 = (bf16[144,1024]{1,0:T(8,128)(2,1)S(1)}, bf16[144,1024]{1,0:T(8,128)(2,1)}, u32[]{:S(2)}, u32[]{:S(2)}) collective-permute-start(bf16[144,1024]{1,0:T(8,128)(2,1)S(1)} %slice.13), channel_id=1, source_target_pairs={{0,6},{1,7},{2,0},{3,1},{4,2},{5,3},{6,4},{7,5},{8,14},{9,15},{10,... | collective-permute-start | bytes 884744 | tf_op jit(solution)/shard_map/ppermute | solution.py:211
  96.4 10.6 %collective-permute-start.3 = (bf16[144,1024]{1,0:T(8,128)(2,1)S(1)}, bf16[144,1024]{1,0:T(8,128)(2,1)}, u32[]{:S(2)}, u32[]{:S(2)}) collective-permute-start(bf16[144,1024]{1,0:T(8,128)(2,1)S(1)} %slice.12), channel_id=1, source_target_pairs={{0,2},{1,3},{2,4},{3,5},{4,6},{5,7},{6,0},{7,1},{8,10},{9,11},{10,... | collective-permute-start | bytes 884744 | tf_op jit(solution)/shard_map/ppermute | solution.py:211
  99.0 12.0 %collective-permute-start.7 = (bf16[288,1024]{1,0:T(8,128)(2,1)S(1)}, bf16[288,1024]{1,0:T(8,128)(2,1)S(1)}, u32[]{:S(2)}, u32[]{:S(2)}) collective-permute-start(bf16[288,1024]{1,0:T(8,128)(2,1)S(1)} %collective-permute-done.2.refs_2_), channel_id=1, source_target_pairs={{0,1},{1,0},{2,3},{3,2},{4,5},{5,4},{6,7},{7,6},{8,9},{9,8},{10,11... | collective-permute-start | bytes 1769480 | tf_op jit(solution)/shard_map/ppermute | solution.py:211
  102.0 10.5 %collective-permute-start.6 = (bf16[288,1024]{1,0:T(8,128)(2,1)S(1)}, bf16[288,1024]{1,0:T(8,128)(2,1)S(1)}, u32[]{:S(2)}, u32[]{:S(2)}) collective-permute-start(bf16[288,1024]{1,0:T(8,128)(2,1)S(1)} %collective-permute-done.1.refs_1_), channel_id=1, source_target_pairs={{0,1},{1,0},{2,3},{3,2},{4,5},{5,4},{6,7},{7,6},{8,9},{9,8},{10,11... | collective-permute-start | bytes 1769480 | tf_op jit(solution)/shard_map/ppermute | solution.py:211
  103.9 7.0 %collective-permute-start.9 = (bf16[144,1024]{1,0:T(8,128)(2,1)}, bf16[144,1024]{1,0:T(8,128)(2,1)}, u32[]{:S(2)}, u32[]{:S(2)}) collective-permute-start(bf16[144,1024]{1,0:T(8,128)(2,1)} %collective-permute-done.4.refs_4_), channel_id=1, source_target_pairs={{0,1},{1,0},{2,3},{3,2},{4,5},{5,4},{6,7},{7,6},{8,9},{9,8},{10,11... | collective-permute-start | bytes 884744 | tf_op jit(solution)/shard_map/ppermute | solution.py:211
  107.0 5.5 %collective-permute-start.8 = (bf16[144,1024]{1,0:T(8,128)(2,1)}, bf16[144,1024]{1,0:T(8,128)(2,1)}, u32[]{:S(2)}, u32[]{:S(2)}) collective-permute-start(bf16[144,1024]{1,0:T(8,128)(2,1)} %collective-permute-done.3.refs_3_), channel_id=1, source_target_pairs={{0,1},{1,0},{2,3},{3,2},{4,5},{5,4},{6,7},{7,6},{8,9},{9,8},{10,11... | collective-permute-start | bytes 884744 | tf_op jit(solution)/shard_map/ppermute | solution.py:211

commit v3 on v2

v3 whole, which is shorter than its diff:
```python
import math

import jax
import jax.numpy as jnp
from jax import lax
from jax.experimental import pallas as pl
from jax.experimental.pallas import tpu as pltpu
from jax.sharding import PartitionSpec as P

TAPS = 4
L = 2048
G = 64
C = 6
Q = 12
I = 16
S = 24
F32, BF16 = jnp.float32, jnp.bfloat16
PARAMS = pltpu.CompilerParams(vmem_limit_bytes=24 * 1024 * 1024)
VMEM = pl.BlockSpec(memory_space=pltpu.VMEM)


def dot(a, b, ca, cb):
    return lax.dot_general(a, b, (((ca,), (cb,)), ((), ())), preferred_element_type=F32)


def iota(shape, dim):
    return lax.broadcasted_iota(jnp.int32, shape, dim)


def window_table(taps, length_total):
    span = taps * length_total
    t = lax.broadcasted_iota(F32, (taps, length_total), 0)
    m = (taps - 1 - t) * length_total + lax.broadcasted_iota(F32, (taps, length_total), 1)
    return jnp.sinc((m - span / 2.0) / length_total) * (
        0.5 - 0.5 * jnp.cos(2.0 * math.pi * m / span)
    )


def cosine(m):
    r = jnp.abs(((m + L // 2) & (L - 1)) - L // 2)
    flip = r > L // 4
    r = jnp.where(flip, L // 2 - r, r)
    u = r.astype(F32) * (2.0 * math.pi / L)
    u = u * u
    acc = jnp.full_like(u, 1.0 / math.factorial(14) * -1.0)
    for k in range(6, -1, -1):
        acc = acc * u + (-1.0) ** k / math.factorial(2 * k)
    return jnp.where(flip, -acc, acc)


def tail_kernel(samples_ref, out_ref):
    out_ref[...] = samples_ref[:, S - 8 :, :].astype(F32)[:, 4:, :].astype(BF16)


def table_kernel(kept_ref, table_ref, swap_ref):
    rows = 2 * G * 4
    r = iota((rows, 1), 0)
    owner = (r // 4) % 2 * (G // 2) + (r // 8) % 32
    tail = r >= G * 4
    want = owner * C + jnp.where(tail, 4 + r % 2, r % 4)
    keep = kept_ref.shape[0]
    chan = jnp.sum(
        jnp.where(iota((rows, keep), 1) == want, kept_ref[...].astype(F32).reshape(1, keep), 0.0), axis=1, keepdims=True
    ).astype(jnp.int32)
    turn = jnp.where(tail, (r // 2) % 2 * (L // 4), 0)
    lane = iota((rows, 128), 1)
    step = chan * 128
    cs = cosine(step + jnp.where(lane < 64, 0, 3 * (L // 4)))
    first = chan * lane + turn
    re0, im0 = cosine(first), cosine(first + 3 * (L // 4))
    half = G * 4
    for n in range(0, rows, 64):
        at = slice(n, n + 64)
        re, im = re0[at], im0[at]
        ca, sa = jnp.broadcast_to(cs[at, 0:1], (64, 128)), jnp.broadcast_to(cs[at, 64:65], (64, 128))
        place = n if n < half else n + half
        for h in range(L // 128):
            cols = slice(h * 128, (h + 1) * 128)
            table_ref[place : place + 64, cols] = re.astype(BF16)
            if n < half:
                table_ref[half + n : half + n + 64, cols] = (-im).astype(BF16)
            re, im = re * ca - im * sa, re * sa + im * ca
    n = 1024
    col = iota((1, 128), 1)
    base = iota((n, 128), 0) - ((col // 16) * 128 + col % 16)
    for h in range(n // 128):
        swap_ref[:, h * 128 : (h + 1) * 128] = jnp.where(base == h * 16, 1.0, 0.0).astype(BF16)


def spectra_kernel(table_ref, samples_ref, halo_ref, weights_ref, out_ref, filtered):
    step = 512
    row = iota((8, step), 0)

    def fir(pair, carry):
        for n in range(0, L, step):
            cols = slice(n, n + step)
            parts = []
            for one in range(2):
                i = pair * 2 + one
                now = samples_ref[i, :, cols].astype(F32)
                back = halo_ref[i, :, cols].astype(F32)
                back = jnp.concatenate([back, back], axis=0)
                total = weights_ref[0:1, cols] * now
                for d in range(1, TAPS):
                    moved = pltpu.roll(now, d, 0)
                    head = jnp.where(row < d, pltpu.roll(back, d, 0), moved[0:8])
                    moved = jnp.concatenate([head, moved[8:]], axis=0)
                    total = total + weights_ref[d : d + 1, cols] * moved
                parts.append(total)
            both = jnp.concatenate(parts, axis=0).astype(BF16)
            filtered[pl.ds(pl.multiple_of(pair * 2 * S, 2 * S), 2 * S), cols] = both
        return carry

    lax.fori_loop(0, I // 2, fir, 0)
    width = I * S
    col = iota((width, width), 1)
    order = jnp.where(iota((width, width), 0) == (col % I) * S + col // I, 1.0, 0.0).astype(BF16)
    scale = 1.0 / math.sqrt(L)

    def transform(first):
        value = dot(table_ref[first : first + 256, :], filtered[...], 1, 1) * scale
        value = dot(value.astype(BF16), order, 1, 0)
        return value.reshape(32, 8, width)

    for m in range(3):
        value = transform(m * 256).astype(BF16)
        out_ref[0:32, :, m * width : (m + 1) * width] = value[:, 0:4]
        out_ref[32:64, :, m * width : (m + 1) * width] = value[:, 4:8]


def regroup_kernel(owned_ref, swap_ref, all_ref, low_ref, high_ref, rows_ref, wide_ref):
    units = 36
    for g in range(G):
        big, small = g // 8, g % 8
        for t in range(9):
            place = big * 40 + t * 4
            rows_ref[place : place + 4, small * 128 : (small + 1) * 128] = owned_ref[
                g, :, t * 128 : (t + 1) * 128
            ].astype(F32)
    for s in range(8):
        wide_ref[s * 40 + 32 : s * 40 + 40, :] = jnp.zeros((8, 1024), F32)
    rows = rows_ref[...].astype(BF16)
    for h in range(4):
        part = dot(rows, swap_ref[:, h * 256 : (h + 1) * 256], 1, 0)
        for big in range(8):
            for s in range(2):
                place = (h * 2 + s) * 40
                wide_ref[place : place + units, big * 128 : (big + 1) * 128] = part[
                    big * 40 : big * 40 + units, s * 128 : (s + 1) * 128
                ]
    shape = (Q * S, 320)
    r = iota(shape, 0)
    q, s = r // S, r % S
    c, p = q // 2, q % 2
    m = jnp.where(c < 4, p, 2)
    unit = (m * 3 + s // 8) * 4 + jnp.where(c < 4, c, p * 2 + c - 4)
    order = jnp.where(iota(shape, 1) == (s % 8) * 40 + unit, 1.0, 0.0).astype(BF16)
    mine = dot(order, wide_ref[...].astype(BF16), 1, 0).astype(BF16)
    all_ref[...] = mine
    low_ref[...] = mine[: Q * S // 2]
    high_ref[...] = mine[Q * S // 2 :]


PER = C // 2


def correlate_kernel(block_ref, *refs):
    mine, up_low, down_low, far_low, up_high, down_high, far_high, first_o, last_o, out_ref = refs
    first = pl.multiple_of(block_ref[0] * 128, 128)
    depth = 2 * S
    mid = PER * depth

    def run(places):
        for one in range(PER):
            left, other, right = [], [], []
            for ref, base in places:
                rows = slice(base + one * depth, base + (one + 1) * depth)
                v = ref[rows, pl.ds(first, 128)].astype(F32)
                left.append(v)
                other += [v[S:], -v[:S]]
                right.append(ref[rows, :])
            right = jnp.concatenate(right, axis=0)
            left = jnp.concatenate(
                [jnp.concatenate(left, axis=0), jnp.concatenate(other, axis=0)], axis=1
            )
            total = dot(left.astype(BF16), right, 0, 0) * (1.0 / (8 * S))
            out_ref[one] = total.reshape(2, 128, 1024).astype(BF16)

    @pl.when(pl.program_id(0) == 0)
    def _():
        run([(mine, 0), (up_low, 0), (down_low, 0), (far_low, 0)]
            + [(first_o, 0), (first_o, 2 * mid), (last_o, 0), (last_o, 2 * mid)])

    @pl.when(pl.program_id(0) == 1)
    def _():
        run([(mine, mid), (up_high, 0), (down_high, 0), (far_high, 0)]
            + [(first_o, mid), (first_o, 3 * mid), (last_o, mid), (last_o, 3 * mid)])


def local(samples, kept):
    block = lax.axis_index("tblk").reshape(1)
    steps = lax.axis_size("tblk")
    tail = pl.pallas_call(
        tail_kernel,
        out_shape=jax.ShapeDtypeStruct((I, 4, L), BF16),
        in_specs=[VMEM],
        out_specs=VMEM,
        compiler_params=PARAMS,
    )(samples)
    halo = lax.ppermute(tail, "tblk", [(i, i + 1) for i in range(steps - 1)])
    weights = window_table(TAPS, L)
    table, swap = pl.pallas_call(
        table_kernel,
        out_shape=[
            jax.ShapeDtypeStruct((G * Q, L), BF16),
            jax.ShapeDtypeStruct((1024, 1024), BF16),
        ],
        in_specs=[VMEM],
        out_specs=[VMEM, VMEM],
        compiler_params=PARAMS,
        cost_estimate=pl.CostEstimate(flops=10_000_000, bytes_accessed=20_000_000, transcendentals=0),
    )(kept)
    chunks = pl.pallas_call(
        spectra_kernel,
        out_shape=jax.ShapeDtypeStruct((G, 4, 1152), BF16),
        in_specs=[VMEM] * 4,
        out_specs=VMEM,
        scratch_shapes=[pltpu.VMEM((I * S, L), BF16)],
        compiler_params=PARAMS,
    )(table, samples, halo, weights)
    owned = lax.all_to_all(chunks, "inp", split_axis=0, concat_axis=0, tiled=True)
    rows = Q * S
    mine, low, high = pl.pallas_call(
        regroup_kernel,
        out_shape=[jax.ShapeDtypeStruct((n, 1024), BF16) for n in (rows, rows // 2, rows // 2)],
        in_specs=[VMEM] * 2,
        out_specs=[VMEM] * 3,
        scratch_shapes=[pltpu.VMEM((320, 1024), F32), pltpu.VMEM((320, 1024), F32)],
        compiler_params=PARAMS,
    )(owned, swap)
    send = lambda v, hop: lax.ppermute(v, "tblk", [(i, (i + hop) % steps) for i in range(steps)])
    flip = lambda *v: lax.ppermute(
        jnp.concatenate(v, axis=0), "tblk", [(i, i ^ 1) for i in range(steps)]
    )
    up_low, down_high = send(low, 2), send(high, -2)
    up_high, down_low = send(high, 2), send(low, -2)
    far_low, far_high = send(up_low, 2), send(down_high, -2)
    first_o = flip(mine, up_low, down_high)
    last_o = flip(down_low, up_high, far_low, far_high)
    return pl.pallas_call(
        correlate_kernel,
        out_shape=jax.ShapeDtypeStruct((C, 2, 128, 1024), BF16),
        grid_spec=pltpu.PrefetchScalarGridSpec(
            num_scalar_prefetch=1,
            grid=(C // PER,),
            in_specs=[VMEM] * 9,
            out_specs=pl.BlockSpec((PER, 2, 128, 1024), lambda c, b: (c, 0, 0, 0)),
        ),
        compiler_params=PARAMS,
    )(block, mine, up_low, down_low, far_low, up_high, down_high, far_high, first_o, last_o)


def solution(mesh):
    placed = (P("inp", "tblk", None), P())
    return jax.shard_map(
        local, mesh=mesh, in_specs=placed, out_specs=P("inp", None, "tblk", None), check_vma=False
    )
```

time: 119 us -> 107 us (0.90)
  waiting for transfers between devices: 11.4 us -> 6.02 us
  Pallas kernels: 17.6 us -> 13 us
  blocking collectives: 56.4 us -> 52.7 us
  other arithmetic: 0.33 us -> 2.6 us
  local copies, waits for them, and re-layouts: 3.73 us -> 2.09 us
  starting transfers between devices: 28.9 us -> 30.4 us
    ppermute x10 -> x9, waiting for transfers between devices: 11.4 us -> 6.02 us  [the longest x2 2.78 us: local(): lax.ppermute(jnp.concatenate(v, axis=0), 'tblk', [(i, i ^ 1) for i in ran...]
    all_to_all x1, blocking collectives: 56.4 us -> 52.7 us  [local(): lax.all_to_all(chunks, 'inp', split_axis=0, concat_axis=0, tiled=True)]
    pallas_call x1, Pallas kernels: 5.69 us -> 2.62 us  [local(): pl.pallas_call(table_kernel, out_shape=[jax.ShapeDtypeStruct((G * Q, L),...]
    concatenate x0 -> x2, other arithmetic: none -> 2.2 us  [local(): jnp.concatenate(v, axis=0)]
    pallas_call x1, Pallas kernels: 6.15 us -> 4.47 us  [local(): pl.pallas_call(correlate_kernel, out_shape=jax.ShapeDtypeStruct((C, 2, 12...]
    ppermute x10 -> x9, starting transfers between devices: 28.9 us -> 30.4 us  [the longest x6 18.3 us: local(): lax.ppermute(v, 'tblk', [(i, (i + hop) % steps) for i in range(steps)])]
    slice x3 -> x0, local copies, waits for them, and re-layouts: 1.23 us -> none  [the longest x1 1.19 us: local(): samples[:, S - 4:, :]]
    pallas_call x2 -> x3, Pallas kernels: 5.77 us -> 5.88 us  [the longest x1 4.37 us: local(): pl.pallas_call(spectra_kernel, out_shape=jax.ShapeDtypeStruct((G, 4, 1152...]
  transfers between devices with their start and end apart: 10 -> 9, of which waited for: 3 -> 4; matrix products, arithmetic and copies ran while one was open for 1% -> 2% of each run, Pallas kernels for 5% -> 2%
where the time goes in v3:
time: 107 us
  blocking collectives  52.7 us (49%)
  starting transfers between devices  30.4 us (28%)
  Pallas kernels  13 us (12%)
  waiting for transfers between devices  6.02 us (6%)
  other arithmetic  2.6 us (2%)
  local copies, waits for them, and re-layouts  2.09 us (2%)
    all_to_all x1, blocking collectives, local(): lax.all_to_all(chunks, 'inp', split_axis=0, concat_axis=0, tiled=True)  52.7 us
    ppermute x6, starting transfers between devices, local(): lax.ppermute(v, 'tblk', [(i, (i + hop) % steps) for i in range(steps)])  18.3 us
    ppermute x2, starting transfers between devices, local(): lax.ppermute(jnp.concatenate(v, axis=0), 'tblk', [(i, i ^ 1) for i in ran...  7.47 us
    ppermute x1, starting transfers between devices, local(): halo = lax.ppermute(tail, 'tblk', [(i, i + 1) for i in range(steps - 1)])  4.64 us
    pallas_call x1, Pallas kernels, local(): pl.pallas_call(correlate_kernel, out_shape=jax.ShapeDtypeStruct((C, 2, 12...  4.47 us
    pallas_call x1, Pallas kernels, local(): pl.pallas_call(spectra_kernel, out_shape=jax.ShapeDtypeStruct((G, 4, 1152...  4.37 us
    ppermute x2, waiting for transfers between devices, local(): lax.ppermute(jnp.concatenate(v, axis=0), 'tblk', [(i, i ^ 1) for i in ran...  2.78 us
    pallas_call x1, Pallas kernels, local(): pl.pallas_call(table_kernel, out_shape=[jax.ShapeDtypeStruct((G * Q, L),...  2.62 us
  transfers between devices with their start and end apart: 9, of which 4 were waited for; matrix products, arithmetic and copies ran while one was open for 2% of the time, Pallas kernels for 2%

profile of v3, /device:TPU:1, one launch (start us, length us, event | category | flops | bytes accessed | tf_op | source)
XLA Modules:
  0.0 106.9 jit_solution(16168451993854984636)
XLA Ops:
  0.0 0.0 copy-start
  0.0 1.4 %copy-done = bf16[16,24,2048]{2,1,0:T(8,128)(2,1)S(1)} copy-done((bf16[16,24,2048]{2,1,0:T(8,128)(2,1)S(1)}, bf16[16,24,2048]{2,1,0:T(8,128)(2,1)}, u32[]{:S(2)}) %copy-start) | copy-done | bytes 1572888
  1.4 0.0 copy-start.1
  1.4 0.1 shard_map.29
  1.5 4.6 %collective-permute-start = (bf16[16,4,2048]{2,1,0:T(4,128)(2,1)S(1)}, bf16[16,4,2048]{2,1,0:T(4,128)(2,1)S(1)}, u32[]{:S(2)}, u32[]{:S(2)}) collective-permute-start(bf16[16,4,2048]{2,1,0:T(4,128)(2,1)S(1)} %shard_map.29), channel_id=1, source_target_pairs={{0,1},{1,2},{2,3},{3,4},{4,5},{5,6},{6,7},{8,9},{9,10},{10,11},{11... | collective-permute-start | bytes 786440 | tf_op jit(solution)/shard_map/ppermute | solution.py:210
  6.1 0.0 copy-start.2
  6.1 0.7 copy-done.2
  6.8 2.6 %shard_map.28 = (bf16[768,2048]{1,0:T(8,128)(2,1)S(1)}, bf16[1024,1024]{1,0:T(8,128)(2,1)S(1)}) custom-call(s32[384]{0:T(512)S(1)} %copy-done.2), custom_call_target="tpu_custom_call" | custom-call | flops 10000000 | bytes 20000000 | tf_op jit(solution)/shard_map/pallas_call | solution.py:212
  9.4 0.4 fusion.5.weights_ref
  9.8 0.9 collective-permute-done.halo_ref
  10.8 0.0 copy-done.1
  10.8 4.4 %shard_map.30 = bf16[64,4,1152]{2,1,0:T(4,128)(2,1)S(1)} custom-call(bf16[768,2048]{1,0:T(8,128)(2,1)S(1)} %get-tuple-element.10.table_ref, bf16[16,24,2048]{2,1,0:T(8,128)(2,1)S(1)} %copy-done.1, bf16[16,4,2048]{2,1,0:T(4,128)(2,1)S(1)} %collective-permute-done.halo_ref, f32[4,2048]{1,0:T(4,128)S(1)} %fusion.5.weights_ref), custom_call_target="tpu_custom_call" | custom-call | tf_op jit(solution)/shard_map/pallas_call | solution.py:223
  15.2 52.7 %all_to_all.5.owned_ref = bf16[64,4,1152]{2,1,0:T(4,128)(2,1)S(1)} all-to-all(bf16[64,4,1152]{2,1,0:T(4,128)(2,1)S(1)} %shard_map.30), channel_id=1, replica_groups=mesh['inp'=64,'tblk'=8] {'inp'}, dimensions={0} | all-to-all | bytes 1179648 | tf_op jit(solution)/shard_map/all_to_all | solution.py:231
  67.9 1.5 %shard_map.31 = (bf16[288,1024]{1,0:T(8,128)(2,1)S(1)}, bf16[144,1024]{1,0:T(8,128)(2,1)S(1)}, bf16[144,1024]{1,0:T(8,128)(2,1)S(1)}) custom-call(bf16[64,4,1152]{2,1,0:T(4,128)(2,1)S(1)} %all_to_all.5.owned_ref, bf16[1024,1024]{1,0:T(8,128)(2,1)S(1)} %get-tuple-element.11.swap_ref), custom_call_target="tpu_custom_call" | custom-call | tf_op jit(solution)/shard_map/pallas_call | solution.py:233
  69.3 1.9 %collective-permute-start.1 = (bf16[144,1024]{1,0:T(8,128)(2,1)S(1)}, bf16[144,1024]{1,0:T(8,128)(2,1)S(1)}, u32[]{:S(2)}, u32[]{:S(2)}) collective-permute-start(bf16[144,1024]{1,0:T(8,128)(2,1)S(1)} %get-tuple-element.13), channel_id=1, source_target_pairs={{0,2},{1,3},{2,4},{3,5},{4,6},{5,7},{6,0},{7,1},{8,10},{9,11},{10,... | collective-permute-start | bytes 884744 | tf_op jit(solution)/shard_map/ppermute | solution.py:241
  71.3 4.6 %collective-permute-start.5 = (bf16[144,1024]{1,0:T(8,128)(2,1)S(1)}, bf16[144,1024]{1,0:T(8,128)(2,1)S(1)}, u32[]{:S(2)}, u32[]{:S(2)}) collective-permute-start(bf16[144,1024]{1,0:T(8,128)(2,1)S(1)} %get-tuple-element.14), channel_id=1, source_target_pairs={{0,6},{1,7},{2,0},{3,1},{4,2},{5,3},{6,4},{7,5},{8,14},{9,15},{10,... | collective-permute-start | bytes 884744 | tf_op jit(solution)/shard_map/ppermute | solution.py:241
  75.9 1.9 %collective-permute-start.2 = (bf16[144,1024]{1,0:T(8,128)(2,1)S(1)}, bf16[144,1024]{1,0:T(8,128)(2,1)S(1)}, u32[]{:S(2)}, u32[]{:S(2)}) collective-permute-start(bf16[144,1024]{1,0:T(8,128)(2,1)S(1)} %get-tuple-element.13), channel_id=1, source_target_pairs={{0,6},{1,7},{2,0},{3,1},{4,2},{5,3},{6,4},{7,5},{8,14},{9,15},{10,... | collective-permute-start | bytes 884744 | tf_op jit(solution)/shard_map/ppermute | solution.py:241
  77.8 3.4 %collective-permute-start.4 = (bf16[144,1024]{1,0:T(8,128)(2,1)S(1)}, bf16[144,1024]{1,0:T(8,128)(2,1)S(1)}, u32[]{:S(2)}, u32[]{:S(2)}) collective-permute-start(bf16[144,1024]{1,0:T(8,128)(2,1)S(1)} %get-tuple-element.14), channel_id=1, source_target_pairs={{0,2},{1,3},{2,4},{3,5},{4,6},{5,7},{6,0},{7,1},{8,10},{9,11},{10,... | collective-permute-start | bytes 884744 | tf_op jit(solution)/shard_map/ppermute | solution.py:241
  81.2 0.0 collective-permute-done.1.refs_1_
  81.2 1.9 %collective-permute-start.3 = (bf16[144,1024]{1,0:T(8,128)(2,1)S(1)}, bf16[144,1024]{1,0:T(8,128)(2,1)S(1)}, u32[]{:S(2)}, u32[]{:S(2)}) collective-permute-start(bf16[144,1024]{1,0:T(8,128)(2,1)S(1)} %collective-permute-done.1.refs_1_), channel_id=1, source_target_pairs={{0,2},{1,3},{2,4},{3,5},{4,6},{5,7},{6,0},{7,1},{8,10},{9,11},{10,... | collective-permute-start | bytes 884744 | tf_op jit(solution)/shard_map/ppermute | solution.py:241
  83.1 0.0 collective-permute-done.5.refs_5_
  83.1 4.6 %collective-permute-start.6 = (bf16[144,1024]{1,0:T(8,128)(2,1)S(1)}, bf16[144,1024]{1,0:T(8,128)(2,1)S(1)}, u32[]{:S(2)}, u32[]{:S(2)}) collective-permute-start(bf16[144,1024]{1,0:T(8,128)(2,1)S(1)} %collective-permute-done.5.refs_5_), channel_id=1, source_target_pairs={{0,6},{1,7},{2,0},{3,1},{4,2},{5,3},{6,4},{7,5},{8,14},{9,15},{10,... | collective-permute-start | bytes 884744 | tf_op jit(solution)/shard_map/ppermute | solution.py:241
  87.7 1.1 %pad_maximum_fusion = bf16[576,1024]{1,0:T(8,128)(2,1)} fusion(bf16[144,1024]{1,0:T(8,128)(2,1)S(1)} %collective-permute-done.5.refs_5_, bf16[144,1024]{1,0:T(8,128)(2,1)S(1)} %collective-permute-done.1.refs_1_, bf16[288,1024]{1,0:T(8,128)(2,1)S(1)} %get-tuple-element.12.refs_0_), kind=kLoop, calls=%fused_computation | loop fusion | flops 3538944 | bytes 2359296 | tf_op jit(solution)/shard_map/concatenate | solution.py:243
  88.8 3.3 %collective-permute-start.7 = (bf16[576,1024]{1,0:T(8,128)(2,1)}, bf16[576,1024]{1,0:T(8,128)(2,1)S(1)}, u32[]{:S(2)}, u32[]{:S(2)}) collective-permute-start(bf16[576,1024]{1,0:T(8,128)(2,1)} %pad_maximum_fusion), channel_id=1, source_target_pairs={{0,1},{1,0},{2,3},{3,2},{4,5},{5,4},{6,7},{7,6},{8,9},{9,8},{10,11... | collective-permute-start | bytes 3538952 | tf_op jit(solution)/shard_map/ppermute | solution.py:242
  92.2 0.0 collective-permute-done.2.refs_2_
  92.2 0.0 collective-permute-done.4.refs_4_
  92.2 1.7 %collective-permute-done.3.refs_3_ = bf16[144,1024]{1,0:T(8,128)(2,1)S(1)} collective-permute-done((bf16[144,1024]{1,0:T(8,128)(2,1)S(1)}, bf16[144,1024]{1,0:T(8,128)(2,1)S(1)}, u32[]{:S(2)}, u32[]{:S(2)}) %collective-permute-start.3) | collective-permute-done | bytes 294944 | tf_op jit(solution)/shard_map/ppermute | solution.py:241
  93.9 0.5 collective-permute-done.6.refs_6_
  94.4 1.1 %pad_maximum_fusion.1 = bf16[576,1024]{1,0:T(8,128)(2,1)} fusion(bf16[144,1024]{1,0:T(8,128)(2,1)S(1)} %collective-permute-done.6.refs_6_, bf16[144,1024]{1,0:T(8,128)(2,1)S(1)} %collective-permute-done.3.refs_3_, bf16[144,1024]{1,0:T(8,128)(2,1)S(1)} %collective-permute-done.4.refs_4_, bf16[144,1024]{1,0:T(8,128)(2,1)S(1)} %collective-permute-done.2.refs_2_), kind=kLoop, calls=%fused_computation.1 | loop fusion | flops 4718592 | bytes 2359296 | tf_op jit(solution)/shard_map/concatenate | solution.py:243
  95.5 4.1 %collective-permute-start.8 = (bf16[576,1024]{1,0:T(8,128)(2,1)}, bf16[576,1024]{1,0:T(8,128)(2,1)}, u32[]{:S(2)}, u32[]{:S(2)}) collective-permute-start(bf16[576,1024]{1,0:T(8,128)(2,1)} %pad_maximum_fusion.1), channel_id=1, source_target_pairs={{0,1},{1,0},{2,3},{3,2},{4,5},{5,4},{6,7},{7,6},{8,9},{9,8},{10,11... | collective-permute-start | bytes 3538952 | tf_op jit(solution)/shard_map/ppermute | solution.py:242
  99.7 0.0 collective-permute-done.7.refs_7_
  99.7 2.8 %collective-permute-done.8.refs_8_ = bf16[576,1024]{1,0:T(8,128)(2,1)} collective-permute-done((bf16[576,1024]{1,0:T(8,128)(2,1)}, bf16[576,1024]{1,0:T(8,128)(2,1)}, u32[]{:S(2)}, u32[]{:S(2)}) %collective-permute-start.8) | collective-permute-done | bytes 1179680 | tf_op jit(solution)/shard_map/ppermute | solution.py:242
  102.5 4.5 %shard_map.32 = bf16[6,2,128,1024]{3,2,1,0:T(8,128)(2,1)} custom-call(s32[1]{0:T(128)} %bitcast.block_ref, bf16[288,1024]{1,0:T(8,128)(2,1)S(1)} %get-tuple-element.12.refs_0_, bf16[144,1024]{1,0:T(8,128)(2,1)S(1)} %collective-permute-done.1.refs_1_, bf16[144,1024]{1,0:T(8,128)(2,1)S(1)} %collective-permute-done.2.refs_2_, ...), custom_call_target="tpu_custom_call" | custom-call | tf_op jit(solution)/shard_map/pallas_call | solution.py:250
  (1 shorter events, 0.0 us)
Async XLA Ops:
  0.0 1.4 %copy-start = (bf16[16,24,2048]{2,1,0:T(8,128)(2,1)S(1)}, bf16[16,24,2048]{2,1,0:T(8,128)(2,1)}, u32[]{:S(2)}) copy-start(bf16[16,24,2048]{2,1,0:T(8,128)(2,1)} %samples_ref.3) | copy-start | bytes 4718596
  1.4 9.4 %copy-start.1 = (bf16[16,24,2048]{2,1,0:T(8,128)(2,1)S(1)}, bf16[16,24,2048]{2,1,0:T(8,128)(2,1)}, u32[]{:S(2)}) copy-start(bf16[16,24,2048]{2,1,0:T(8,128)(2,1)} %samples_ref.3) | copy-start | bytes 4718596
  1.5 9.3 %collective-permute-start = (bf16[16,4,2048]{2,1,0:T(4,128)(2,1)S(1)}, bf16[16,4,2048]{2,1,0:T(4,128)(2,1)S(1)}, u32[]{:S(2)}, u32[]{:S(2)}) collective-permute-start(bf16[16,4,2048]{2,1,0:T(4,128)(2,1)S(1)} %shard_map.29), channel_id=1, source_target_pairs={{0,1},{1,2},{2,3},{3,4},{4,5},{5,6},{6,7},{8,9},{9,10},{10,11},{11... | collective-permute-start | bytes 786440 | tf_op jit(solution)/shard_map/ppermute | solution.py:210
  6.1 0.7 copy-start.2
  69.3 11.9 %collective-permute-start.1 = (bf16[144,1024]{1,0:T(8,128)(2,1)S(1)}, bf16[144,1024]{1,0:T(8,128)(2,1)S(1)}, u32[]{:S(2)}, u32[]{:S(2)}) collective-permute-start(bf16[144,1024]{1,0:T(8,128)(2,1)S(1)} %get-tuple-element.13), channel_id=1, source_target_pairs={{0,2},{1,3},{2,4},{3,5},{4,6},{5,7},{6,0},{7,1},{8,10},{9,11},{10,... | collective-permute-start | bytes 884744 | tf_op jit(solution)/shard_map/ppermute | solution.py:241
  71.3 11.9 %collective-permute-start.5 = (bf16[144,1024]{1,0:T(8,128)(2,1)S(1)}, bf16[144,1024]{1,0:T(8,128)(2,1)S(1)}, u32[]{:S(2)}, u32[]{:S(2)}) collective-permute-start(bf16[144,1024]{1,0:T(8,128)(2,1)S(1)} %get-tuple-element.14), channel_id=1, source_target_pairs={{0,6},{1,7},{2,0},{3,1},{4,2},{5,3},{6,4},{7,5},{8,14},{9,15},{10,... | collective-permute-start | bytes 884744 | tf_op jit(solution)/shard_map/ppermute | solution.py:241
  75.9 16.3 %collective-permute-start.2 = (bf16[144,1024]{1,0:T(8,128)(2,1)S(1)}, bf16[144,1024]{1,0:T(8,128)(2,1)S(1)}, u32[]{:S(2)}, u32[]{:S(2)}) collective-permute-start(bf16[144,1024]{1,0:T(8,128)(2,1)S(1)} %get-tuple-element.13), channel_id=1, source_target_pairs={{0,6},{1,7},{2,0},{3,1},{4,2},{5,3},{6,4},{7,5},{8,14},{9,15},{10,... | collective-permute-start | bytes 884744 | tf_op jit(solution)/shard_map/ppermute | solution.py:241
  77.8 14.4 %collective-permute-start.4 = (bf16[144,1024]{1,0:T(8,128)(2,1)S(1)}, bf16[144,1024]{1,0:T(8,128)(2,1)S(1)}, u32[]{:S(2)}, u32[]{:S(2)}) collective-permute-start(bf16[144,1024]{1,0:T(8,128)(2,1)S(1)} %get-tuple-element.14), channel_id=1, source_target_pairs={{0,2},{1,3},{2,4},{3,5},{4,6},{5,7},{6,0},{7,1},{8,10},{9,11},{10,... | collective-permute-start | bytes 884744 | tf_op jit(solution)/shard_map/ppermute | solution.py:241
  81.2 12.7 %collective-permute-start.3 = (bf16[144,1024]{1,0:T(8,128)(2,1)S(1)}, bf16[144,1024]{1,0:T(8,128)(2,1)S(1)}, u32[]{:S(2)}, u32[]{:S(2)}) collective-permute-start(bf16[144,1024]{1,0:T(8,128)(2,1)S(1)} %collective-permute-done.1.refs_1_), channel_id=1, source_target_pairs={{0,2},{1,3},{2,4},{3,5},{4,6},{5,7},{6,0},{7,1},{8,10},{9,11},{10,... | collective-permute-start | bytes 884744 | tf_op jit(solution)/shard_map/ppermute | solution.py:241
  83.1 11.3 %collective-permute-start.6 = (bf16[144,1024]{1,0:T(8,128)(2,1)S(1)}, bf16[144,1024]{1,0:T(8,128)(2,1)S(1)}, u32[]{:S(2)}, u32[]{:S(2)}) collective-permute-start(bf16[144,1024]{1,0:T(8,128)(2,1)S(1)} %collective-permute-done.5.refs_5_), channel_id=1, source_target_pairs={{0,6},{1,7},{2,0},{3,1},{4,2},{5,3},{6,4},{7,5},{8,14},{9,15},{10,... | collective-permute-start | bytes 884744 | tf_op jit(solution)/shard_map/ppermute | solution.py:241
  88.8 10.8 %collective-permute-start.7 = (bf16[576,1024]{1,0:T(8,128)(2,1)}, bf16[576,1024]{1,0:T(8,128)(2,1)S(1)}, u32[]{:S(2)}, u32[]{:S(2)}) collective-permute-start(bf16[576,1024]{1,0:T(8,128)(2,1)} %pad_maximum_fusion), channel_id=1, source_target_pairs={{0,1},{1,0},{2,3},{3,2},{4,5},{5,4},{6,7},{7,6},{8,9},{9,8},{10,11... | collective-permute-start | bytes 3538952 | tf_op jit(solution)/shard_map/ppermute | solution.py:242
  95.5 6.9 %collective-permute-start.8 = (bf16[576,1024]{1,0:T(8,128)(2,1)}, bf16[576,1024]{1,0:T(8,128)(2,1)}, u32[]{:S(2)}, u32[]{:S(2)}) collective-permute-start(bf16[576,1024]{1,0:T(8,128)(2,1)} %pad_maximum_fusion.1), channel_id=1, source_target_pairs={{0,1},{1,0},{2,3},{3,2},{4,5},{5,4},{6,7},{7,6},{8,9},{9,8},{10,11... | collective-permute-start | bytes 3538952 | tf_op jit(solution)/shard_map/ppermute | solution.py:242

commit v4 on v3

--- a/solution.py
+++ b/solution.py
@@ -15,7 +15,7 @@
 I = 16
 S = 24
 F32, BF16 = jnp.float32, jnp.bfloat16
-PARAMS = pltpu.CompilerParams(vmem_limit_bytes=24 * 1024 * 1024)
+PARAMS = pltpu.CompilerParams(vmem_limit_bytes=16 * 1024 * 1024)
 VMEM = pl.BlockSpec(memory_space=pltpu.VMEM)
 
 
@@ -48,8 +48,9 @@
     return jnp.where(flip, -acc, acc)
 
 
-def tail_kernel(samples_ref, out_ref):
+def tail_kernel(samples_ref, kept_ref, out_ref, kept_out):
     out_ref[...] = samples_ref[:, S - 8 :, :].astype(F32)[:, 4:, :].astype(BF16)
+    kept_out[...] = kept_ref[...].astype(F32).reshape(1, kept_ref.shape[0])
 
 
 def table_kernel(kept_ref, table_ref, swap_ref):
@@ -58,9 +59,9 @@
     owner = (r // 4) % 2 * (G // 2) + (r // 8) % 32
     tail = r >= G * 4
     want = owner * C + jnp.where(tail, 4 + r % 2, r % 4)
-    keep = kept_ref.shape[0]
+    keep = kept_ref.shape[1]
     chan = jnp.sum(
-        jnp.where(iota((rows, keep), 1) == want, kept_ref[...].astype(F32).reshape(1, keep), 0.0), axis=1, keepdims=True
+        jnp.where(iota((rows, keep), 1) == want, kept_ref[...], 0.0), axis=1, keepdims=True
     ).astype(jnp.int32)
     turn = jnp.where(tail, (r // 2) % 2 * (L // 4), 0)
     lane = iota((rows, 128), 1)
@@ -161,52 +162,63 @@
     high_ref[...] = mine[Q * S // 2 :]
 
 
-PER = C // 2
-
-
-def correlate_kernel(block_ref, *refs):
-    mine, up_low, down_low, far_low, up_high, down_high, far_high, first_o, last_o, out_ref = refs
+MID = C // 2
+DEPTH = 2 * S
+
+
+def products(first, places, one):
+    left, other, right = [], [], []
+    for ref, base in places:
+        rows = slice(base + one * DEPTH, base + (one + 1) * DEPTH)
+        v = ref[rows, pl.ds(first, 128)].astype(F32)
+        left.append(v)
+        other += [v[S:], -v[:S]]
+        right.append(ref[rows, :])
+    left = jnp.concatenate([jnp.concatenate(left, axis=0), jnp.concatenate(other, axis=0)], axis=1)
+    return dot(left.astype(BF16), jnp.concatenate(right, axis=0), 0, 0) * (1.0 / (8 * S))
+
+
+def places(first, last, high):
+    half = MID * DEPTH
+    at = half if high else 0
+    return [(first, at), (first, 2 * half + at), (last, at), (last, 2 * half + at)]
+
+
+def pack_kernel(*refs):
+    at = 0
+    for ref in refs[:-1]:
+        refs[-1][at : at + ref.shape[0]] = ref[...]
+        at += ref.shape[0]
+
+
+def own_kernel(block_ref, first_ref, last_ref, out_ref):
     first = pl.multiple_of(block_ref[0] * 128, 128)
-    depth = 2 * S
-    mid = PER * depth
-
-    def run(places):
-        for one in range(PER):
-            left, other, right = [], [], []
-            for ref, base in places:
-                rows = slice(base + one * depth, base + (one + 1) * depth)
-                v = ref[rows, pl.ds(first, 128)].astype(F32)
-                left.append(v)
-                other += [v[S:], -v[:S]]
-                right.append(ref[rows, :])
-            right = jnp.concatenate(right, axis=0)
-            left = jnp.concatenate(
-                [jnp.concatenate(left, axis=0), jnp.concatenate(other, axis=0)], axis=1
-            )
-            total = dot(left.astype(BF16), right, 0, 0) * (1.0 / (8 * S))
-            out_ref[one] = total.reshape(2, 128, 1024).astype(BF16)
-
-    @pl.when(pl.program_id(0) == 0)
-    def _():
-        run([(mine, 0), (up_low, 0), (down_low, 0), (far_low, 0)]
-            + [(first_o, 0), (first_o, 2 * mid), (last_o, 0), (last_o, 2 * mid)])
-
-    @pl.when(pl.program_id(0) == 1)
-    def _():
-        run([(mine, mid), (up_high, 0), (down_high, 0), (far_high, 0)]
-            + [(first_o, mid), (first_o, 3 * mid), (last_o, mid), (last_o, 3 * mid)])
+    for c in range(C):
+        out_ref[c] = products(first, places(first_ref, last_ref, c >= MID), c % MID)
+
+
+def other_kernel(block_ref, first_ref, last_ref, part_ref, out_ref):
+    first = pl.multiple_of(block_ref[0] * 128, 128)
+    for high in range(2):
+
+        @pl.when(pl.program_id(0) == high)
+        def _():
+            for one in range(MID):
+                total = products(first, places(first_ref, last_ref, high), one)
+                total = total + part_ref[high * MID + one]
+                out_ref[one] = total.reshape(2, 128, 1024).astype(BF16)
 
 
 def local(samples, kept):
     block = lax.axis_index("tblk").reshape(1)
     steps = lax.axis_size("tblk")
-    tail = pl.pallas_call(
+    tail, channels = pl.pallas_call(
         tail_kernel,
-        out_shape=jax.ShapeDtypeStruct((I, 4, L), BF16),
-        in_specs=[VMEM],
-        out_specs=VMEM,
-        compiler_params=PARAMS,
-    )(samples)
+        out_shape=[jax.ShapeDtypeStruct((I, 4, L), BF16), jax.ShapeDtypeStruct((1, kept.shape[0]), F32)],
+        in_specs=[VMEM] * 2,
+        out_specs=[VMEM] * 2,
+        compiler_params=PARAMS,
+    )(samples, kept)
     halo = lax.ppermute(tail, "tblk", [(i, i + 1) for i in range(steps - 1)])
     weights = window_table(TAPS, L)
     table, swap = pl.pallas_call(
@@ -219,7 +231,7 @@
         out_specs=[VMEM, VMEM],
         compiler_params=PARAMS,
         cost_estimate=pl.CostEstimate(flops=10_000_000, bytes_accessed=20_000_000, transcendentals=0),
-    )(kept)
+    )(channels)
     chunks = pl.pallas_call(
         spectra_kernel,
         out_shape=jax.ShapeDtypeStruct((G, 4, 1152), BF16),
@@ -239,25 +251,43 @@
         compiler_params=PARAMS,
     )(owned, swap)
     send = lambda v, hop: lax.ppermute(v, "tblk", [(i, (i + hop) % steps) for i in range(steps)])
-    flip = lambda *v: lax.ppermute(
-        jnp.concatenate(v, axis=0), "tblk", [(i, i ^ 1) for i in range(steps)]
-    )
+    flip = lambda v: lax.ppermute(v, "tblk", [(i, i ^ 1) for i in range(steps)])
+
+    def pack(*parts):
+        return pl.pallas_call(
+            pack_kernel,
+            out_shape=pltpu.VMEM((2 * rows, 1024), BF16),
+            in_specs=[VMEM] * len(parts),
+            out_specs=VMEM,
+            compiler_params=PARAMS,
+        )(*parts)
+
     up_low, down_high = send(low, 2), send(high, -2)
     up_high, down_low = send(high, 2), send(low, -2)
     far_low, far_high = send(up_low, 2), send(down_high, -2)
-    first_o = flip(mine, up_low, down_high)
-    last_o = flip(down_low, up_high, far_low, far_high)
+    near = pack(mine, up_low, down_high)
+    near_o = flip(near)
+    rest = pack(down_low, up_high, far_low, far_high)
+    rest_o = flip(rest)
+    part = pl.pallas_call(
+        own_kernel,
+        out_shape=pltpu.VMEM((C, 256, 1024), F32),
+        in_specs=[pl.BlockSpec(memory_space=pltpu.SMEM)] + [VMEM] * 2,
+        out_specs=VMEM,
+        compiler_params=PARAMS,
+        cost_estimate=pl.CostEstimate(flops=600_000_000, bytes_accessed=9_000_000, transcendentals=0),
+    )(block, near, rest)
     return pl.pallas_call(
-        correlate_kernel,
+        other_kernel,
         out_shape=jax.ShapeDtypeStruct((C, 2, 128, 1024), BF16),
         grid_spec=pltpu.PrefetchScalarGridSpec(
             num_scalar_prefetch=1,
-            grid=(C // PER,),
-            in_specs=[VMEM] * 9,
-            out_specs=pl.BlockSpec((PER, 2, 128, 1024), lambda c, b: (c, 0, 0, 0)),
+            grid=(2,),
+            in_specs=[VMEM] * 3,
+            out_specs=pl.BlockSpec((MID, 2, 128, 1024), lambda c, b: (c, 0, 0, 0)),
         ),
         compiler_params=PARAMS,
-    )(block, mine, up_low, down_low, far_low, up_high, down_high, far_high, first_o, last_o)
+    )(block, near_o, rest_o, part)
 
 
 def solution(mesh):

time: 107 us -> 105 us (0.981)
  other arithmetic: 2.6 us -> 0.4 us
    concatenate x2 -> x0, other arithmetic: 2.2 us -> none  [local(): jnp.concatenate(v, axis=0)]
    ppermute x6, waiting for transfers between devices: 2.29 us -> 3.58 us  [local(): lax.ppermute(v, 'tblk', [(i, (i + hop) % steps) for i in range(steps)])]
    ppermute x2, waiting for transfers between devices: 2.78 us -> 1.54 us  [local(): flip = lambda v: lax.ppermute(v, 'tblk', [(i, i ^ 1) for i in range(steps)])]
    pallas_call x2 -> x5, Pallas kernels: 4.52 us -> 4.93 us  [the longest x1 3.69 us: local(): pl.pallas_call(other_kernel, out_shape=jax.ShapeDtypeStruct((C, 2, 128, 1...]
  transfers between devices with their start and end apart: 9 -> 9, of which waited for: 4 -> 5; matrix products, arithmetic and copies ran while one was open for 2% -> 0% of each run, Pallas kernels for 2% -> 4%
where the time goes in v4:
time: 105 us
  blocking collectives  52 us (50%)
  starting transfers between devices  30.1 us (29%)
  Pallas kernels  13.4 us (13%)
  waiting for transfers between devices  6.75 us (6%)
  local copies, waits for them, and re-layouts  2.09 us (2%)
    all_to_all x1, blocking collectives, local(): lax.all_to_all(chunks, 'inp', split_axis=0, concat_axis=0, tiled=True)  52 us
    ppermute x6, starting transfers between devices, local(): lax.ppermute(v, 'tblk', [(i, (i + hop) % steps) for i in range(steps)])  18.3 us
    ppermute x2, starting transfers between devices, local(): flip = lambda v: lax.ppermute(v, 'tblk', [(i, i ^ 1) for i in range(steps)])  7.2 us
    ppermute x1, starting transfers between devices, local(): halo = lax.ppermute(tail, 'tblk', [(i, i + 1) for i in range(steps - 1)])  4.64 us
    pallas_call x1, Pallas kernels, local(): pl.pallas_call(spectra_kernel, out_shape=jax.ShapeDtypeStruct((G, 4, 1152...  4.37 us
    pallas_call x1, Pallas kernels, local(): pl.pallas_call(other_kernel, out_shape=jax.ShapeDtypeStruct((C, 2, 128, 1...  3.69 us
    ppermute x6, waiting for transfers between devices, local(): lax.ppermute(v, 'tblk', [(i, (i + hop) % steps) for i in range(steps)])  3.58 us
    pallas_call x1, Pallas kernels, local(): pl.pallas_call(table_kernel, out_shape=[jax.ShapeDtypeStruct((G * Q, L),...  2.61 us
  transfers between devices with their start and end apart: 9, of which 5 were waited for; matrix products, arithmetic and copies ran while one was open for 0% of the time, Pallas kernels for 4%

profile of v4, /device:TPU:1, one launch (start us, length us, event | category | flops | bytes accessed | tf_op | source)
XLA Modules:
  0.0 104.9 jit_solution(4292402986975837887)
XLA Ops:
  0.0 0.0 copy-start
  0.0 1.4 %copy-done = bf16[16,24,2048]{2,1,0:T(8,128)(2,1)S(1)} copy-done((bf16[16,24,2048]{2,1,0:T(8,128)(2,1)S(1)}, bf16[16,24,2048]{2,1,0:T(8,128)(2,1)}, u32[]{:S(2)}) %copy-start) | copy-done | bytes 1572888
  1.4 0.0 copy-start.2
  1.4 0.7 copy-done.2
  2.1 0.0 copy-start.1
  2.1 0.1 shard_map.28
  2.1 4.6 %collective-permute-start = (bf16[16,4,2048]{2,1,0:T(4,128)(2,1)S(1)}, bf16[16,4,2048]{2,1,0:T(4,128)(2,1)S(1)}, u32[]{:S(2)}, u32[]{:S(2)}) collective-permute-start(bf16[16,4,2048]{2,1,0:T(4,128)(2,1)S(1)} %get-tuple-element.14), channel_id=1, source_target_pairs={{0,1},{1,2},{2,3},{3,4},{4,5},{5,6},{6,7},{8,9},{9,10},{10,11},{11... | collective-permute-start | bytes 786440 | tf_op jit(solution)/shard_map/ppermute | solution.py:222
  6.8 2.6 %shard_map.29 = (bf16[768,2048]{1,0:T(8,128)(2,1)S(1)}, bf16[1024,1024]{1,0:T(8,128)(2,1)S(1)}) custom-call(f32[1,384]{1,0:T(1,128)S(1)} %get-tuple-element.12.kept_ref), custom_call_target="tpu_custom_call" | custom-call | flops 10000000 | bytes 20000000 | tf_op jit(solution)/shard_map/pallas_call | solution.py:224
  9.4 0.4 fusion.5.weights_ref
  9.8 1.6 %collective-permute-done.halo_ref = bf16[16,4,2048]{2,1,0:T(4,128)(2,1)S(1)} collective-permute-done((bf16[16,4,2048]{2,1,0:T(4,128)(2,1)S(1)}, bf16[16,4,2048]{2,1,0:T(4,128)(2,1)S(1)}, u32[]{:S(2)}, u32[]{:S(2)}) %collective-permute-start) | collective-permute-done | bytes 262176 | tf_op jit(solution)/shard_map/ppermute | solution.py:222
  11.5 0.0 copy-done.1
  11.5 4.4 %shard_map.30 = bf16[64,4,1152]{2,1,0:T(4,128)(2,1)S(1)} custom-call(bf16[768,2048]{1,0:T(8,128)(2,1)S(1)} %get-tuple-element.13.table_ref, bf16[16,24,2048]{2,1,0:T(8,128)(2,1)S(1)} %copy-done.1, bf16[16,4,2048]{2,1,0:T(4,128)(2,1)S(1)} %collective-permute-done.halo_ref, f32[4,2048]{1,0:T(4,128)S(1)} %fusion.5.weights_ref), custom_call_target="tpu_custom_call" | custom-call | tf_op jit(solution)/shard_map/pallas_call | solution.py:235
  15.8 52.0 %all_to_all.5.owned_ref = bf16[64,4,1152]{2,1,0:T(4,128)(2,1)S(1)} all-to-all(bf16[64,4,1152]{2,1,0:T(4,128)(2,1)S(1)} %shard_map.30), channel_id=1, replica_groups=mesh['inp'=64,'tblk'=8] {'inp'}, dimensions={0} | all-to-all | bytes 1179648 | tf_op jit(solution)/shard_map/all_to_all | solution.py:243
  67.9 1.5 %shard_map.31 = (bf16[288,1024]{1,0:T(8,128)(2,1)S(1)}, bf16[144,1024]{1,0:T(8,128)(2,1)S(1)}, bf16[144,1024]{1,0:T(8,128)(2,1)S(1)}) custom-call(bf16[64,4,1152]{2,1,0:T(4,128)(2,1)S(1)} %all_to_all.5.owned_ref, bf16[1024,1024]{1,0:T(8,128)(2,1)S(1)} %get-tuple-element.15.swap_ref), custom_call_target="tpu_custom_call" | custom-call | tf_op jit(solution)/shard_map/pallas_call | solution.py:245
  69.3 1.9 %collective-permute-start.1 = (bf16[144,1024]{1,0:T(8,128)(2,1)S(1)}, bf16[144,1024]{1,0:T(8,128)(2,1)S(1)}, u32[]{:S(2)}, u32[]{:S(2)}) collective-permute-start(bf16[144,1024]{1,0:T(8,128)(2,1)S(1)} %get-tuple-element.17), channel_id=1, source_target_pairs={{0,2},{1,3},{2,4},{3,5},{4,6},{5,7},{6,0},{7,1},{8,10},{9,11},{10,... | collective-permute-start | bytes 884744 | tf_op jit(solution)/shard_map/ppermute | solution.py:253
  71.3 4.6 %collective-permute-start.2 = (bf16[144,1024]{1,0:T(8,128)(2,1)S(1)}, bf16[144,1024]{1,0:T(8,128)(2,1)S(1)}, u32[]{:S(2)}, u32[]{:S(2)}) collective-permute-start(bf16[144,1024]{1,0:T(8,128)(2,1)S(1)} %get-tuple-element.18), channel_id=1, source_target_pairs={{0,6},{1,7},{2,0},{3,1},{4,2},{5,3},{6,4},{7,5},{8,14},{9,15},{10,... | collective-permute-start | bytes 884744 | tf_op jit(solution)/shard_map/ppermute | solution.py:253
  75.8 1.9 %collective-permute-start.4 = (bf16[144,1024]{1,0:T(8,128)(2,1)S(1)}, bf16[144,1024]{1,0:T(8,128)(2,1)S(1)}, u32[]{:S(2)}, u32[]{:S(2)}) collective-permute-start(bf16[144,1024]{1,0:T(8,128)(2,1)S(1)} %get-tuple-element.17), channel_id=1, source_target_pairs={{0,6},{1,7},{2,0},{3,1},{4,2},{5,3},{6,4},{7,5},{8,14},{9,15},{10,... | collective-permute-start | bytes 884744 | tf_op jit(solution)/shard_map/ppermute | solution.py:253
  77.8 3.4 %collective-permute-start.5 = (bf16[144,1024]{1,0:T(8,128)(2,1)S(1)}, bf16[144,1024]{1,0:T(8,128)(2,1)S(1)}, u32[]{:S(2)}, u32[]{:S(2)}) collective-permute-start(bf16[144,1024]{1,0:T(8,128)(2,1)S(1)} %get-tuple-element.18), channel_id=1, source_target_pairs={{0,2},{1,3},{2,4},{3,5},{4,6},{5,7},{6,0},{7,1},{8,10},{9,11},{10,... | collective-permute-start | bytes 884744 | tf_op jit(solution)/shard_map/ppermute | solution.py:253
  81.1 0.2 collective-permute-done.1.refs_1_
  81.3 1.9 %collective-permute-start.6 = (bf16[144,1024]{1,0:T(8,128)(2,1)S(1)}, bf16[144,1024]{1,0:T(8,128)(2,1)S(1)}, u32[]{:S(2)}, u32[]{:S(2)}) collective-permute-start(bf16[144,1024]{1,0:T(8,128)(2,1)S(1)} %collective-permute-done.1.refs_1_), channel_id=1, source_target_pairs={{0,2},{1,3},{2,4},{3,5},{4,6},{5,7},{6,0},{7,1},{8,10},{9,11},{10,... | collective-permute-start | bytes 884744 | tf_op jit(solution)/shard_map/ppermute | solution.py:253
  83.3 0.0 collective-permute-done.2.refs_2_
  83.3 4.6 %collective-permute-start.7 = (bf16[144,1024]{1,0:T(8,128)(2,1)S(1)}, bf16[144,1024]{1,0:T(8,128)(2,1)S(1)}, u32[]{:S(2)}, u32[]{:S(2)}) collective-permute-start(bf16[144,1024]{1,0:T(8,128)(2,1)S(1)} %collective-permute-done.2.refs_2_), channel_id=1, source_target_pairs={{0,6},{1,7},{2,0},{3,1},{4,2},{5,3},{6,4},{7,5},{8,14},{9,15},{10,... | collective-permute-start | bytes 884744 | tf_op jit(solution)/shard_map/ppermute | solution.py:253
  87.8 0.1 shard_map.32.first_ref
  87.9 3.1 %collective-permute-start.3 = (bf16[576,1024]{1,0:T(8,128)(2,1)S(1)}, bf16[576,1024]{1,0:T(8,128)(2,1)S(1)}, u32[]{:S(2)}, u32[]{:S(2)}) collective-permute-start(bf16[576,1024]{1,0:T(8,128)(2,1)S(1)} %shard_map.32.first_ref), channel_id=1, source_target_pairs={{0,1},{1,0},{2,3},{3,2},{4,5},{5,4},{6,7},{7,6},{8,9},{9,8},{10,11... | collective-permute-start | bytes 3538952 | tf_op jit(solution)/shard_map/ppermute | solution.py:254
  91.1 0.0 collective-permute-done.4.refs_0_
  91.1 0.0 collective-permute-done.5.refs_1_
  91.1 2.5 %collective-permute-done.6.refs_2_ = bf16[144,1024]{1,0:T(8,128)(2,1)S(1)} collective-permute-done((bf16[144,1024]{1,0:T(8,128)(2,1)S(1)}, bf16[144,1024]{1,0:T(8,128)(2,1)S(1)}, u32[]{:S(2)}, u32[]{:S(2)}) %collective-permute-start.6) | collective-permute-done | bytes 294944 | tf_op jit(solution)/shard_map/ppermute | solution.py:253
  93.6 0.8 collective-permute-done.7.refs_3_
  94.5 0.1 shard_map.33.last_ref
  94.5 4.1 %collective-permute-start.8 = (bf16[576,1024]{1,0:T(8,128)(2,1)S(1)}, bf16[576,1024]{1,0:T(8,128)(2,1)}, u32[]{:S(2)}, u32[]{:S(2)}) collective-permute-start(bf16[576,1024]{1,0:T(8,128)(2,1)S(1)} %shard_map.33.last_ref), channel_id=1, source_target_pairs={{0,1},{1,0},{2,3},{3,2},{4,5},{5,4},{6,7},{7,6},{8,9},{9,8},{10,11... | collective-permute-start | bytes 3538952 | tf_op jit(solution)/shard_map/ppermute | solution.py:254
  98.6 1.0 shard_map.34.part_ref
  99.7 0.0 collective-permute-done.3.first_ref
  99.7 1.5 %collective-permute-done.8.last_ref = bf16[576,1024]{1,0:T(8,128)(2,1)} collective-permute-done((bf16[576,1024]{1,0:T(8,128)(2,1)S(1)}, bf16[576,1024]{1,0:T(8,128)(2,1)}, u32[]{:S(2)}, u32[]{:S(2)}) %collective-permute-start.8) | collective-permute-done | bytes 1179680 | tf_op jit(solution)/shard_map/ppermute | solution.py:254
  101.2 3.7 %shard_map.35 = bf16[6,2,128,1024]{3,2,1,0:T(8,128)(2,1)} custom-call(s32[1]{0:T(128)} %bitcast.block_ref, bf16[576,1024]{1,0:T(8,128)(2,1)S(1)} %collective-permute-done.3.first_ref, bf16[576,1024]{1,0:T(8,128)(2,1)} %collective-permute-done.8.last_ref, f32[6,256,1024]{2,1,0:T(8,128)S(1)} %shard_map.34.part_ref), custom_call_target="tpu_custom_call" | custom-call | tf_op jit(solution)/shard_map/pallas_call | solution.py:280
  (1 shorter events, 0.0 us)
Async XLA Ops:
  0.0 1.4 %copy-start = (bf16[16,24,2048]{2,1,0:T(8,128)(2,1)S(1)}, bf16[16,24,2048]{2,1,0:T(8,128)(2,1)}, u32[]{:S(2)}) copy-start(bf16[16,24,2048]{2,1,0:T(8,128)(2,1)} %samples_ref.3) | copy-start | bytes 4718596
  1.4 0.7 copy-start.2
  2.1 9.4 %copy-start.1 = (bf16[16,24,2048]{2,1,0:T(8,128)(2,1)S(1)}, bf16[16,24,2048]{2,1,0:T(8,128)(2,1)}, u32[]{:S(2)}) copy-start(bf16[16,24,2048]{2,1,0:T(8,128)(2,1)} %samples_ref.3) | copy-start | bytes 4718596
  2.1 9.3 %collective-permute-start = (bf16[16,4,2048]{2,1,0:T(4,128)(2,1)S(1)}, bf16[16,4,2048]{2,1,0:T(4,128)(2,1)S(1)}, u32[]{:S(2)}, u32[]{:S(2)}) collective-permute-start(bf16[16,4,2048]{2,1,0:T(4,128)(2,1)S(1)} %get-tuple-element.14), channel_id=1, source_target_pairs={{0,1},{1,2},{2,3},{3,4},{4,5},{5,6},{6,7},{8,9},{9,10},{10,11},{11... | collective-permute-start | bytes 786440 | tf_op jit(solution)/shard_map/ppermute | solution.py:222
  69.3 12.0 %collective-permute-start.1 = (bf16[144,1024]{1,0:T(8,128)(2,1)S(1)}, bf16[144,1024]{1,0:T(8,128)(2,1)S(1)}, u32[]{:S(2)}, u32[]{:S(2)}) collective-permute-start(bf16[144,1024]{1,0:T(8,128)(2,1)S(1)} %get-tuple-element.17), channel_id=1, source_target_pairs={{0,2},{1,3},{2,4},{3,5},{4,6},{5,7},{6,0},{7,1},{8,10},{9,11},{10,... | collective-permute-start | bytes 884744 | tf_op jit(solution)/shard_map/ppermute | solution.py:253
  71.3 12.0 %collective-permute-start.2 = (bf16[144,1024]{1,0:T(8,128)(2,1)S(1)}, bf16[144,1024]{1,0:T(8,128)(2,1)S(1)}, u32[]{:S(2)}, u32[]{:S(2)}) collective-permute-start(bf16[144,1024]{1,0:T(8,128)(2,1)S(1)} %get-tuple-element.18), channel_id=1, source_target_pairs={{0,6},{1,7},{2,0},{3,1},{4,2},{5,3},{6,4},{7,5},{8,14},{9,15},{10,... | collective-permute-start | bytes 884744 | tf_op jit(solution)/shard_map/ppermute | solution.py:253
  75.8 15.2 %collective-permute-start.4 = (bf16[144,1024]{1,0:T(8,128)(2,1)S(1)}, bf16[144,1024]{1,0:T(8,128)(2,1)S(1)}, u32[]{:S(2)}, u32[]{:S(2)}) collective-permute-start(bf16[144,1024]{1,0:T(8,128)(2,1)S(1)} %get-tuple-element.17), channel_id=1, source_target_pairs={{0,6},{1,7},{2,0},{3,1},{4,2},{5,3},{6,4},{7,5},{8,14},{9,15},{10,... | collective-permute-start | bytes 884744 | tf_op jit(solution)/shard_map/ppermute | solution.py:253
  77.8 13.3 %collective-permute-start.5 = (bf16[144,1024]{1,0:T(8,128)(2,1)S(1)}, bf16[144,1024]{1,0:T(8,128)(2,1)S(1)}, u32[]{:S(2)}, u32[]{:S(2)}) collective-permute-start(bf16[144,1024]{1,0:T(8,128)(2,1)S(1)} %get-tuple-element.18), channel_id=1, source_target_pairs={{0,2},{1,3},{2,4},{3,5},{4,6},{5,7},{6,0},{7,1},{8,10},{9,11},{10,... | collective-permute-start | bytes 884744 | tf_op jit(solution)/shard_map/ppermute | solution.py:253
  81.3 12.3 %collective-permute-start.6 = (bf16[144,1024]{1,0:T(8,128)(2,1)S(1)}, bf16[144,1024]{1,0:T(8,128)(2,1)S(1)}, u32[]{:S(2)}, u32[]{:S(2)}) collective-permute-start(bf16[144,1024]{1,0:T(8,128)(2,1)S(1)} %collective-permute-done.1.refs_1_), channel_id=1, source_target_pairs={{0,2},{1,3},{2,4},{3,5},{4,6},{5,7},{6,0},{7,1},{8,10},{9,11},{10,... | collective-permute-start | bytes 884744 | tf_op jit(solution)/shard_map/ppermute | solution.py:253
  83.3 11.2 %collective-permute-start.7 = (bf16[144,1024]{1,0:T(8,128)(2,1)S(1)}, bf16[144,1024]{1,0:T(8,128)(2,1)S(1)}, u32[]{:S(2)}, u32[]{:S(2)}) collective-permute-start(bf16[144,1024]{1,0:T(8,128)(2,1)S(1)} %collective-permute-done.2.refs_2_), channel_id=1, source_target_pairs={{0,6},{1,7},{2,0},{3,1},{4,2},{5,3},{6,4},{7,5},{8,14},{9,15},{10,... | collective-permute-start | bytes 884744 | tf_op jit(solution)/shard_map/ppermute | solution.py:253
  87.9 11.7 %collective-permute-start.3 = (bf16[576,1024]{1,0:T(8,128)(2,1)S(1)}, bf16[576,1024]{1,0:T(8,128)(2,1)S(1)}, u32[]{:S(2)}, u32[]{:S(2)}) collective-permute-start(bf16[576,1024]{1,0:T(8,128)(2,1)S(1)} %shard_map.32.first_ref), channel_id=1, source_target_pairs={{0,1},{1,0},{2,3},{3,2},{4,5},{5,4},{6,7},{7,6},{8,9},{9,8},{10,11... | collective-permute-start | bytes 3538952 | tf_op jit(solution)/shard_map/ppermute | solution.py:254
  94.5 6.7 %collective-permute-start.8 = (bf16[576,1024]{1,0:T(8,128)(2,1)S(1)}, bf16[576,1024]{1,0:T(8,128)(2,1)}, u32[]{:S(2)}, u32[]{:S(2)}) collective-permute-start(bf16[576,1024]{1,0:T(8,128)(2,1)S(1)} %shard_map.33.last_ref), channel_id=1, source_target_pairs={{0,1},{1,0},{2,3},{3,2},{4,5},{5,4},{6,7},{7,6},{8,9},{9,8},{10,11... | collective-permute-start | bytes 3538952 | tf_op jit(solution)/shard_map/ppermute | solution.py:254

commit v5 on v4

--- a/solution.py
+++ b/solution.py
@@ -90,7 +90,6 @@
 
 def spectra_kernel(table_ref, samples_ref, halo_ref, weights_ref, out_ref, filtered):
     step = 512
-    row = iota((8, step), 0)
 
     def fir(pair, carry):
         for n in range(0, L, step):
@@ -100,13 +99,10 @@
                 i = pair * 2 + one
                 now = samples_ref[i, :, cols].astype(F32)
                 back = halo_ref[i, :, cols].astype(F32)
-                back = jnp.concatenate([back, back], axis=0)
+                frames = jnp.concatenate([back, back, now], axis=0)
                 total = weights_ref[0:1, cols] * now
                 for d in range(1, TAPS):
-                    moved = pltpu.roll(now, d, 0)
-                    head = jnp.where(row < d, pltpu.roll(back, d, 0), moved[0:8])
-                    moved = jnp.concatenate([head, moved[8:]], axis=0)
-                    total = total + weights_ref[d : d + 1, cols] * moved
+                    total = total + weights_ref[d : d + 1, cols] * pltpu.roll(frames, d, 0)[8:]
                 parts.append(total)
             both = jnp.concatenate(parts, axis=0).astype(BF16)
             filtered[pl.ds(pl.multiple_of(pair * 2 * S, 2 * S), 2 * S), cols] = both
@@ -162,14 +158,21 @@
     high_ref[...] = mine[Q * S // 2 :]
 
 
-MID = C // 2
+PER = 3
 DEPTH = 2 * S
 
 
-def products(first, places, one):
+def pack_kernel(*refs):
+    at = 0
+    for ref in refs[:-1]:
+        refs[-1][at : at + ref.shape[0]] = ref[...]
+        at += ref.shape[0]
+
+
+def products(first, blocks, c):
     left, other, right = [], [], []
-    for ref, base in places:
-        rows = slice(base + one * DEPTH, base + (one + 1) * DEPTH)
+    for ref, base in blocks:
+        rows = slice(base + c * DEPTH, base + (c + 1) * DEPTH)
         v = ref[rows, pl.ds(first, 128)].astype(F32)
         left.append(v)
         other += [v[S:], -v[:S]]
@@ -178,35 +181,20 @@
     return dot(left.astype(BF16), jnp.concatenate(right, axis=0), 0, 0) * (1.0 / (8 * S))
 
 
-def places(first, last, high):
-    half = MID * DEPTH
-    at = half if high else 0
-    return [(first, at), (first, 2 * half + at), (last, at), (last, 2 * half + at)]
-
-
-def pack_kernel(*refs):
-    at = 0
-    for ref in refs[:-1]:
-        refs[-1][at : at + ref.shape[0]] = ref[...]
-        at += ref.shape[0]
-
-
-def own_kernel(block_ref, first_ref, last_ref, out_ref):
+def part_kernel(block_ref, near, rest, near_o, out_ref):
     first = pl.multiple_of(block_ref[0] * 128, 128)
+    half = C * DEPTH
+    blocks = [(ref, base) for ref in (near, rest, near_o) for base in (0, half)]
     for c in range(C):
-        out_ref[c] = products(first, places(first_ref, last_ref, c >= MID), c % MID)
-
-
-def other_kernel(block_ref, first_ref, last_ref, part_ref, out_ref):
+        out_ref[c] = products(first, blocks, c)
+
+
+def last_kernel(block_ref, rest_o, part_ref, out_ref):
     first = pl.multiple_of(block_ref[0] * 128, 128)
-    for high in range(2):
-
-        @pl.when(pl.program_id(0) == high)
-        def _():
-            for one in range(MID):
-                total = products(first, places(first_ref, last_ref, high), one)
-                total = total + part_ref[high * MID + one]
-                out_ref[one] = total.reshape(2, 128, 1024).astype(BF16)
+    for one in range(PER):
+        total = products(first, [(rest_o.at[0], 0), (rest_o.at[1], 0)], one)
+        total = total + part_ref[pl.program_id(0) * PER + one]
+        out_ref[one] = total.reshape(2, 128, 1024).astype(BF16)
 
 
 def local(samples, kept):
@@ -256,7 +244,7 @@
     def pack(*parts):
         return pl.pallas_call(
             pack_kernel,
-            out_shape=pltpu.VMEM((2 * rows, 1024), BF16),
+            out_shape=pltpu.VMEM((sum(v.shape[0] for v in parts), 1024), BF16),
             in_specs=[VMEM] * len(parts),
             out_specs=VMEM,
             compiler_params=PARAMS,
@@ -270,24 +258,24 @@
     rest = pack(down_low, up_high, far_low, far_high)
     rest_o = flip(rest)
     part = pl.pallas_call(
-        own_kernel,
+        part_kernel,
         out_shape=pltpu.VMEM((C, 256, 1024), F32),
-        in_specs=[pl.BlockSpec(memory_space=pltpu.SMEM)] + [VMEM] * 2,
+        in_specs=[pl.BlockSpec(memory_space=pltpu.SMEM)] + [VMEM] * 3,
         out_specs=VMEM,
         compiler_params=PARAMS,
         cost_estimate=pl.CostEstimate(flops=600_000_000, bytes_accessed=9_000_000, transcendentals=0),
-    )(block, near, rest)
+    )(block, near, rest, near_o)
     return pl.pallas_call(
-        other_kernel,
+        last_kernel,
         out_shape=jax.ShapeDtypeStruct((C, 2, 128, 1024), BF16),
         grid_spec=pltpu.PrefetchScalarGridSpec(
             num_scalar_prefetch=1,
-            grid=(2,),
-            in_specs=[VMEM] * 3,
-            out_specs=pl.BlockSpec((MID, 2, 128, 1024), lambda c, b: (c, 0, 0, 0)),
+            grid=(C // PER,),
+            in_specs=[pl.BlockSpec((2, PER * DEPTH, 1024), lambda c, b: (0, c, 0)), VMEM],
+            out_specs=pl.BlockSpec((PER, 2, 128, 1024), lambda c, b: (c, 0, 0, 0)),
         ),
         compiler_params=PARAMS,
-    )(block, near_o, rest_o, part)
+    )(block, rest_o.reshape(2, rows, 1024), part)
 
 
 def solution(mesh):

time: 105 us -> 105 us (level)
  no operation moved by 1% of the time
where the time goes in v5:
time: 105 us; the launch traced here: 104 us
  blocking collectives  52 us (50%)
  starting transfers between devices  30.2 us (29%)
  Pallas kernels  13.7 us (13%)
  waiting for transfers between devices  5.9 us (6%)
  local copies, waits for them, and re-layouts  2.09 us (2%)
    all_to_all x1, blocking collectives, local(): lax.all_to_all(chunks, 'inp', split_axis=0, concat_axis=0, tiled=True)  52 us
    ppermute x6, starting transfers between devices, local(): lax.ppermute(v, 'tblk', [(i, (i + hop) % steps) for i in range(steps)])  18.3 us
    ppermute x2, starting transfers between devices, local(): flip = lambda v: lax.ppermute(v, 'tblk', [(i, i ^ 1) for i in range(steps)])  7.25 us
    ppermute x1, starting transfers between devices, local(): halo = lax.ppermute(tail, 'tblk', [(i, i + 1) for i in range(steps - 1)])  4.64 us
    pallas_call x1, Pallas kernels, local(): pl.pallas_call(spectra_kernel, out_shape=jax.ShapeDtypeStruct((G, 4, 1152...  4.19 us
    ppermute x6, waiting for transfers between devices, local(): lax.ppermute(v, 'tblk', [(i, (i + hop) % steps) for i in range(steps)])  3.52 us
    pallas_call x1, Pallas kernels, local(): pl.pallas_call(last_kernel, out_shape=jax.ShapeDtypeStruct((C, 2, 128, 10...  3.43 us
    pallas_call x1, Pallas kernels, local(): pl.pallas_call(table_kernel, out_shape=[jax.ShapeDtypeStruct((G * Q, L),...  2.61 us
  transfers between devices with their start and end apart: 9, of which 5 were waited for; matrix products, arithmetic and copies ran while one was open for 0% of the time, Pallas kernels for 4%

profile of v5, /device:TPU:1, one launch (start us, length us, event | category | flops | bytes accessed | tf_op | source)
XLA Modules:
  0.0 104.5 jit_solution(16596974496779279442)
XLA Ops:
  0.0 0.0 copy-start
  0.0 1.4 %copy-done = bf16[16,24,2048]{2,1,0:T(8,128)(2,1)S(1)} copy-done((bf16[16,24,2048]{2,1,0:T(8,128)(2,1)S(1)}, bf16[16,24,2048]{2,1,0:T(8,128)(2,1)}, u32[]{:S(2)}) %copy-start) | copy-done | bytes 1572888
  1.4 0.0 copy-start.2
  1.4 0.7 copy-done.2
  2.1 0.0 copy-start.1
  2.1 0.1 shard_map.28
  2.1 4.6 %collective-permute-start = (bf16[16,4,2048]{2,1,0:T(4,128)(2,1)S(1)}, bf16[16,4,2048]{2,1,0:T(4,128)(2,1)S(1)}, u32[]{:S(2)}, u32[]{:S(2)}) collective-permute-start(bf16[16,4,2048]{2,1,0:T(4,128)(2,1)S(1)} %get-tuple-element.14), channel_id=1, source_target_pairs={{0,1},{1,2},{2,3},{3,4},{4,5},{5,6},{6,7},{8,9},{9,10},{10,11},{11... | collective-permute-start | bytes 786440 | tf_op jit(solution)/shard_map/ppermute | solution.py:210
  6.8 2.6 %shard_map.29 = (bf16[768,2048]{1,0:T(8,128)(2,1)S(1)}, bf16[1024,1024]{1,0:T(8,128)(2,1)S(1)}) custom-call(f32[1,384]{1,0:T(1,128)S(1)} %get-tuple-element.12.kept_ref), custom_call_target="tpu_custom_call" | custom-call | flops 10000000 | bytes 20000000 | tf_op jit(solution)/shard_map/pallas_call | solution.py:212
  9.4 0.4 fusion.5.weights_ref
  9.8 1.6 %collective-permute-done.halo_ref = bf16[16,4,2048]{2,1,0:T(4,128)(2,1)S(1)} collective-permute-done((bf16[16,4,2048]{2,1,0:T(4,128)(2,1)S(1)}, bf16[16,4,2048]{2,1,0:T(4,128)(2,1)S(1)}, u32[]{:S(2)}, u32[]{:S(2)}) %collective-permute-start) | collective-permute-done | bytes 262176 | tf_op jit(solution)/shard_map/ppermute | solution.py:210
  11.5 0.0 copy-done.1
  11.5 4.2 %shard_map.30 = bf16[64,4,1152]{2,1,0:T(4,128)(2,1)S(1)} custom-call(bf16[768,2048]{1,0:T(8,128)(2,1)S(1)} %get-tuple-element.13.table_ref, bf16[16,24,2048]{2,1,0:T(8,128)(2,1)S(1)} %copy-done.1, bf16[16,4,2048]{2,1,0:T(4,128)(2,1)S(1)} %collective-permute-done.halo_ref, f32[4,2048]{1,0:T(4,128)S(1)} %fusion.5.weights_ref), custom_call_target="tpu_custom_call" | custom-call | tf_op jit(solution)/shard_map/pallas_call | solution.py:223
  15.7 52.0 %all_to_all.5.owned_ref = bf16[64,4,1152]{2,1,0:T(4,128)(2,1)S(1)} all-to-all(bf16[64,4,1152]{2,1,0:T(4,128)(2,1)S(1)} %shard_map.30), channel_id=1, replica_groups=mesh['inp'=64,'tblk'=8] {'inp'}, dimensions={0} | all-to-all | bytes 1179648 | tf_op jit(solution)/shard_map/all_to_all | solution.py:231
  67.7 1.5 %shard_map.31 = (bf16[288,1024]{1,0:T(8,128)(2,1)S(1)}, bf16[144,1024]{1,0:T(8,128)(2,1)S(1)}, bf16[144,1024]{1,0:T(8,128)(2,1)S(1)}) custom-call(bf16[64,4,1152]{2,1,0:T(4,128)(2,1)S(1)} %all_to_all.5.owned_ref, bf16[1024,1024]{1,0:T(8,128)(2,1)S(1)} %get-tuple-element.15.swap_ref), custom_call_target="tpu_custom_call" | custom-call | tf_op jit(solution)/shard_map/pallas_call | solution.py:233
  69.2 1.9 %collective-permute-start.3 = (bf16[144,1024]{1,0:T(8,128)(2,1)S(1)}, bf16[144,1024]{1,0:T(8,128)(2,1)S(1)}, u32[]{:S(2)}, u32[]{:S(2)}) collective-permute-start(bf16[144,1024]{1,0:T(8,128)(2,1)S(1)} %get-tuple-element.16), channel_id=1, source_target_pairs={{0,2},{1,3},{2,4},{3,5},{4,6},{5,7},{6,0},{7,1},{8,10},{9,11},{10,... | collective-permute-start | bytes 884744 | tf_op jit(solution)/shard_map/ppermute | solution.py:241
  71.1 4.6 %collective-permute-start.5 = (bf16[144,1024]{1,0:T(8,128)(2,1)S(1)}, bf16[144,1024]{1,0:T(8,128)(2,1)S(1)}, u32[]{:S(2)}, u32[]{:S(2)}) collective-permute-start(bf16[144,1024]{1,0:T(8,128)(2,1)S(1)} %get-tuple-element.17), channel_id=1, source_target_pairs={{0,6},{1,7},{2,0},{3,1},{4,2},{5,3},{6,4},{7,5},{8,14},{9,15},{10,... | collective-permute-start | bytes 884744 | tf_op jit(solution)/shard_map/ppermute | solution.py:241
  75.7 1.9 %collective-permute-start.1 = (bf16[144,1024]{1,0:T(8,128)(2,1)S(1)}, bf16[144,1024]{1,0:T(8,128)(2,1)S(1)}, u32[]{:S(2)}, u32[]{:S(2)}) collective-permute-start(bf16[144,1024]{1,0:T(8,128)(2,1)S(1)} %get-tuple-element.16), channel_id=1, source_target_pairs={{0,6},{1,7},{2,0},{3,1},{4,2},{5,3},{6,4},{7,5},{8,14},{9,15},{10,... | collective-permute-start | bytes 884744 | tf_op jit(solution)/shard_map/ppermute | solution.py:241
  77.6 3.4 %collective-permute-start.2 = (bf16[144,1024]{1,0:T(8,128)(2,1)S(1)}, bf16[144,1024]{1,0:T(8,128)(2,1)S(1)}, u32[]{:S(2)}, u32[]{:S(2)}) collective-permute-start(bf16[144,1024]{1,0:T(8,128)(2,1)S(1)} %get-tuple-element.17), channel_id=1, source_target_pairs={{0,2},{1,3},{2,4},{3,5},{4,6},{5,7},{6,0},{7,1},{8,10},{9,11},{10,... | collective-permute-start | bytes 884744 | tf_op jit(solution)/shard_map/ppermute | solution.py:241
  81.0 0.2 collective-permute-done.3.refs_1_
  81.1 1.9 %collective-permute-start.4 = (bf16[144,1024]{1,0:T(8,128)(2,1)S(1)}, bf16[144,1024]{1,0:T(8,128)(2,1)S(1)}, u32[]{:S(2)}, u32[]{:S(2)}) collective-permute-start(bf16[144,1024]{1,0:T(8,128)(2,1)S(1)} %collective-permute-done.3.refs_1_), channel_id=1, source_target_pairs={{0,2},{1,3},{2,4},{3,5},{4,6},{5,7},{6,0},{7,1},{8,10},{9,11},{10,... | collective-permute-start | bytes 884744 | tf_op jit(solution)/shard_map/ppermute | solution.py:241
  83.0 0.0 collective-permute-done.5.refs_2_
  83.0 4.6 %collective-permute-start.6 = (bf16[144,1024]{1,0:T(8,128)(2,1)S(1)}, bf16[144,1024]{1,0:T(8,128)(2,1)S(1)}, u32[]{:S(2)}, u32[]{:S(2)}) collective-permute-start(bf16[144,1024]{1,0:T(8,128)(2,1)S(1)} %collective-permute-done.5.refs_2_), channel_id=1, source_target_pairs={{0,6},{1,7},{2,0},{3,1},{4,2},{5,3},{6,4},{7,5},{8,14},{9,15},{10,... | collective-permute-start | bytes 884744 | tf_op jit(solution)/shard_map/ppermute | solution.py:241
  87.6 0.1 shard_map.33.near
  87.7 3.2 %collective-permute-start.8 = (bf16[576,1024]{1,0:T(8,128)(2,1)S(1)}, bf16[576,1024]{1,0:T(8,128)(2,1)S(1)}, u32[]{:S(2)}, u32[]{:S(2)}) collective-permute-start(bf16[576,1024]{1,0:T(8,128)(2,1)S(1)} %shard_map.33.near), channel_id=1, source_target_pairs={{0,1},{1,0},{2,3},{3,2},{4,5},{5,4},{6,7},{7,6},{8,9},{9,8},{10,11... | collective-permute-start | bytes 3538952 | tf_op jit(solution)/shard_map/ppermute | solution.py:242
  90.9 0.0 collective-permute-done.1.refs_0_
  90.9 0.0 collective-permute-done.2.refs_1_
  90.9 2.5 %collective-permute-done.4.refs_2_ = bf16[144,1024]{1,0:T(8,128)(2,1)S(1)} collective-permute-done((bf16[144,1024]{1,0:T(8,128)(2,1)S(1)}, bf16[144,1024]{1,0:T(8,128)(2,1)S(1)}, u32[]{:S(2)}, u32[]{:S(2)}) %collective-permute-start.4) | collective-permute-done | bytes 294944 | tf_op jit(solution)/shard_map/ppermute | solution.py:241
  93.5 0.8 collective-permute-done.6.refs_3_
  94.3 0.1 shard_map.32.rest
  94.4 4.1 %collective-permute-start.7 = (bf16[576,1024]{1,0:T(8,128)(2,1)S(1)}, bf16[576,1024]{1,0:T(8,128)(2,1)}, u32[]{:S(2)}, u32[]{:S(2)}) collective-permute-start(bf16[576,1024]{1,0:T(8,128)(2,1)S(1)} %shard_map.32.rest), channel_id=1, source_target_pairs={{0,1},{1,0},{2,3},{3,2},{4,5},{5,4},{6,7},{7,6},{8,9},{9,8},{10,11... | collective-permute-start | bytes 3538952 | tf_op jit(solution)/shard_map/ppermute | solution.py:242
  98.4 0.0 collective-permute-done.8.near_o
  98.5 1.8 %shard_map.34.part_ref = f32[6,256,1024]{2,1,0:T(8,128)S(1)} custom-call(s32[1]{0:T(128)} %bitcast.block_ref, bf16[576,1024]{1,0:T(8,128)(2,1)S(1)} %shard_map.33.near, bf16[576,1024]{1,0:T(8,128)(2,1)S(1)} %shard_map.32.rest, bf16[576,1024]{1,0:T(8,128)(2,1)S(1)} %collective-permute-done.8.near_o), custom_call_target="tpu_custom_call" | custom-call | flops 600000000 | bytes 9000000 | tf_op jit(solution)/shard_map/pallas_call | solution.py:260
  100.3 0.7 collective-permute-done.7
  101.0 3.4 %shard_map.35 = bf16[6,2,128,1024]{3,2,1,0:T(8,128)(2,1)} custom-call(s32[1]{0:T(128)} %bitcast.block_ref, bf16[2,288,1024]{2,1,0:T(8,128)(2,1)} %bitcast.1.rest_o, f32[6,256,1024]{2,1,0:T(8,128)S(1)} %shard_map.34.part_ref), custom_call_target="tpu_custom_call" | custom-call | tf_op jit(solution)/shard_map/pallas_call | solution.py:268
  (1 shorter events, 0.0 us)
Async XLA Ops:
  0.0 1.4 %copy-start = (bf16[16,24,2048]{2,1,0:T(8,128)(2,1)S(1)}, bf16[16,24,2048]{2,1,0:T(8,128)(2,1)}, u32[]{:S(2)}) copy-start(bf16[16,24,2048]{2,1,0:T(8,128)(2,1)} %samples_ref.3) | copy-start | bytes 4718596
  1.4 0.7 copy-start.2
  2.1 9.4 %copy-start.1 = (bf16[16,24,2048]{2,1,0:T(8,128)(2,1)S(1)}, bf16[16,24,2048]{2,1,0:T(8,128)(2,1)}, u32[]{:S(2)}) copy-start(bf16[16,24,2048]{2,1,0:T(8,128)(2,1)} %samples_ref.3) | copy-start | bytes 4718596
  2.1 9.3 %collective-permute-start = (bf16[16,4,2048]{2,1,0:T(4,128)(2,1)S(1)}, bf16[16,4,2048]{2,1,0:T(4,128)(2,1)S(1)}, u32[]{:S(2)}, u32[]{:S(2)}) collective-permute-start(bf16[16,4,2048]{2,1,0:T(4,128)(2,1)S(1)} %get-tuple-element.14), channel_id=1, source_target_pairs={{0,1},{1,2},{2,3},{3,4},{4,5},{5,6},{6,7},{8,9},{9,10},{10,11},{11... | collective-permute-start | bytes 786440 | tf_op jit(solution)/shard_map/ppermute | solution.py:210
  69.2 12.0 %collective-permute-start.3 = (bf16[144,1024]{1,0:T(8,128)(2,1)S(1)}, bf16[144,1024]{1,0:T(8,128)(2,1)S(1)}, u32[]{:S(2)}, u32[]{:S(2)}) collective-permute-start(bf16[144,1024]{1,0:T(8,128)(2,1)S(1)} %get-tuple-element.16), channel_id=1, source_target_pairs={{0,2},{1,3},{2,4},{3,5},{4,6},{5,7},{6,0},{7,1},{8,10},{9,11},{10,... | collective-permute-start | bytes 884744 | tf_op jit(solution)/shard_map/ppermute | solution.py:241
  71.1 11.9 %collective-permute-start.5 = (bf16[144,1024]{1,0:T(8,128)(2,1)S(1)}, bf16[144,1024]{1,0:T(8,128)(2,1)S(1)}, u32[]{:S(2)}, u32[]{:S(2)}) collective-permute-start(bf16[144,1024]{1,0:T(8,128)(2,1)S(1)} %get-tuple-element.17), channel_id=1, source_target_pairs={{0,6},{1,7},{2,0},{3,1},{4,2},{5,3},{6,4},{7,5},{8,14},{9,15},{10,... | collective-permute-start | bytes 884744 | tf_op jit(solution)/shard_map/ppermute | solution.py:241
  75.7 15.2 %collective-permute-start.1 = (bf16[144,1024]{1,0:T(8,128)(2,1)S(1)}, bf16[144,1024]{1,0:T(8,128)(2,1)S(1)}, u32[]{:S(2)}, u32[]{:S(2)}) collective-permute-start(bf16[144,1024]{1,0:T(8,128)(2,1)S(1)} %get-tuple-element.16), channel_id=1, source_target_pairs={{0,6},{1,7},{2,0},{3,1},{4,2},{5,3},{6,4},{7,5},{8,14},{9,15},{10,... | collective-permute-start | bytes 884744 | tf_op jit(solution)/shard_map/ppermute | solution.py:241
  77.6 13.3 %collective-permute-start.2 = (bf16[144,1024]{1,0:T(8,128)(2,1)S(1)}, bf16[144,1024]{1,0:T(8,128)(2,1)S(1)}, u32[]{:S(2)}, u32[]{:S(2)}) collective-permute-start(bf16[144,1024]{1,0:T(8,128)(2,1)S(1)} %get-tuple-element.17), channel_id=1, source_target_pairs={{0,2},{1,3},{2,4},{3,5},{4,6},{5,7},{6,0},{7,1},{8,10},{9,11},{10,... | collective-permute-start | bytes 884744 | tf_op jit(solution)/shard_map/ppermute | solution.py:241
  81.1 12.3 %collective-permute-start.4 = (bf16[144,1024]{1,0:T(8,128)(2,1)S(1)}, bf16[144,1024]{1,0:T(8,128)(2,1)S(1)}, u32[]{:S(2)}, u32[]{:S(2)}) collective-permute-start(bf16[144,1024]{1,0:T(8,128)(2,1)S(1)} %collective-permute-done.3.refs_1_), channel_id=1, source_target_pairs={{0,2},{1,3},{2,4},{3,5},{4,6},{5,7},{6,0},{7,1},{8,10},{9,11},{10,... | collective-permute-start | bytes 884744 | tf_op jit(solution)/shard_map/ppermute | solution.py:241
  83.0 11.2 %collective-permute-start.6 = (bf16[144,1024]{1,0:T(8,128)(2,1)S(1)}, bf16[144,1024]{1,0:T(8,128)(2,1)S(1)}, u32[]{:S(2)}, u32[]{:S(2)}) collective-permute-start(bf16[144,1024]{1,0:T(8,128)(2,1)S(1)} %collective-permute-done.5.refs_2_), channel_id=1, source_target_pairs={{0,6},{1,7},{2,0},{3,1},{4,2},{5,3},{6,4},{7,5},{8,14},{9,15},{10,... | collective-permute-start | bytes 884744 | tf_op jit(solution)/shard_map/ppermute | solution.py:241
  87.7 10.7 %collective-permute-start.8 = (bf16[576,1024]{1,0:T(8,128)(2,1)S(1)}, bf16[576,1024]{1,0:T(8,128)(2,1)S(1)}, u32[]{:S(2)}, u32[]{:S(2)}) collective-permute-start(bf16[576,1024]{1,0:T(8,128)(2,1)S(1)} %shard_map.33.near), channel_id=1, source_target_pairs={{0,1},{1,0},{2,3},{3,2},{4,5},{5,4},{6,7},{7,6},{8,9},{9,8},{10,11... | collective-permute-start | bytes 3538952 | tf_op jit(solution)/shard_map/ppermute | solution.py:242
  94.4 6.7 %collective-permute-start.7 = (bf16[576,1024]{1,0:T(8,128)(2,1)S(1)}, bf16[576,1024]{1,0:T(8,128)(2,1)}, u32[]{:S(2)}, u32[]{:S(2)}) collective-permute-start(bf16[576,1024]{1,0:T(8,128)(2,1)S(1)} %shard_map.32.rest), channel_id=1, source_target_pairs={{0,1},{1,0},{2,3},{3,2},{4,5},{5,4},{6,7},{7,6},{8,9},{9,8},{10,11... | collective-permute-start | bytes 3538952 | tf_op jit(solution)/shard_map/ppermute | solution.py:242

commit v6 on v5

--- a/solution.py
+++ b/solution.py
@@ -53,7 +53,7 @@
     kept_out[...] = kept_ref[...].astype(F32).reshape(1, kept_ref.shape[0])
 
 
-def table_kernel(kept_ref, table_ref, swap_ref):
+def table_kernel(kept_ref, table_ref, swap_ref, stripe_ref):
     rows = 2 * G * 4
     r = iota((rows, 1), 0)
     owner = (r // 4) % 2 * (G // 2) + (r // 8) % 32
@@ -81,11 +81,13 @@
             if n < half:
                 table_ref[half + n : half + n + 64, cols] = (-im).astype(BF16)
             re, im = re * ca - im * sa, re * sa + im * ca
-    n = 1024
+    n, lead = 1024, 112
     col = iota((1, 128), 1)
-    base = iota((n, 128), 0) - ((col // 16) * 128 + col % 16)
+    base = iota((n + lead, 128), 0) - ((col // 16) * 128 + col % 16)
+    stripe_ref[...] = jnp.where(base == lead, 1.0, 0.0).astype(BF16)
     for h in range(n // 128):
-        swap_ref[:, h * 128 : (h + 1) * 128] = jnp.where(base == h * 16, 1.0, 0.0).astype(BF16)
+        at = lead - h * 16
+        swap_ref[:, h * 128 : (h + 1) * 128] = stripe_ref[at : at + n, :]
 
 
 def spectra_kernel(table_ref, samples_ref, halo_ref, weights_ref, out_ref, filtered):
@@ -217,6 +219,7 @@
         ],
         in_specs=[VMEM],
         out_specs=[VMEM, VMEM],
+        scratch_shapes=[pltpu.VMEM((1136, 128), BF16)],
         compiler_params=PARAMS,
         cost_estimate=pl.CostEstimate(flops=10_000_000, bytes_accessed=20_000_000, transcendentals=0),
     )(channels)

time: 105 us -> 105 us (level)
  no operation moved by 1% of the time
where the time goes in v6:
time: 105 us; the launch traced here: 104 us
  blocking collectives  51.7 us (49%)
  starting transfers between devices  30.8 us (29%)
  Pallas kernels  13.4 us (13%)
  waiting for transfers between devices  5.57 us (5%)
  local copies, waits for them, and re-layouts  2.09 us (2%)
    all_to_all x1, blocking collectives, local(): lax.all_to_all(chunks, 'inp', split_axis=0, concat_axis=0, tiled=True)  51.7 us
    ppermute x6, starting transfers between devices, local(): lax.ppermute(v, 'tblk', [(i, (i + hop) % steps) for i in range(steps)])  18.3 us
    ppermute x2, starting transfers between devices, local(): flip = lambda v: lax.ppermute(v, 'tblk', [(i, i ^ 1) for i in range(steps)])  7.93 us
    ppermute x1, starting transfers between devices, local(): halo = lax.ppermute(tail, 'tblk', [(i, i + 1) for i in range(steps - 1)])  4.64 us
    pallas_call x1, Pallas kernels, local(): pl.pallas_call(spectra_kernel, out_shape=jax.ShapeDtypeStruct((G, 4, 1152...  4.19 us
    pallas_call x1, Pallas kernels, local(): pl.pallas_call(last_kernel, out_shape=jax.ShapeDtypeStruct((C, 2, 128, 10...  3.44 us
    ppermute x6, waiting for transfers between devices, local(): lax.ppermute(v, 'tblk', [(i, (i + hop) % steps) for i in range(steps)])  2.84 us
    pallas_call x1, Pallas kernels, local(): pl.pallas_call(table_kernel, out_shape=[jax.ShapeDtypeStruct((G * Q, L),...  2.27 us
  transfers between devices with their start and end apart: 9, of which 5 were waited for; matrix products, arithmetic and copies ran while one was open for 0% of the time, Pallas kernels for 4%

profile of v6, /device:TPU:1, one launch (start us, length us, event | category | flops | bytes accessed | tf_op | source)
XLA Modules:
  0.0 104.1 jit_solution(8687063829468631506)
XLA Ops:
  0.0 0.0 copy-start
  0.0 1.4 %copy-done = bf16[16,24,2048]{2,1,0:T(8,128)(2,1)S(1)} copy-done((bf16[16,24,2048]{2,1,0:T(8,128)(2,1)S(1)}, bf16[16,24,2048]{2,1,0:T(8,128)(2,1)}, u32[]{:S(2)}) %copy-start) | copy-done | bytes 1572888
  1.4 0.0 copy-start.2
  1.4 0.7 copy-done.2
  2.1 0.0 copy-start.1
  2.1 0.1 shard_map.28
  2.1 4.6 %collective-permute-start = (bf16[16,4,2048]{2,1,0:T(4,128)(2,1)S(1)}, bf16[16,4,2048]{2,1,0:T(4,128)(2,1)S(1)}, u32[]{:S(2)}, u32[]{:S(2)}) collective-permute-start(bf16[16,4,2048]{2,1,0:T(4,128)(2,1)S(1)} %get-tuple-element.14), channel_id=1, source_target_pairs={{0,1},{1,2},{2,3},{3,4},{4,5},{5,6},{6,7},{8,9},{9,10},{10,11},{11... | collective-permute-start | bytes 786440 | tf_op jit(solution)/shard_map/ppermute | solution.py:212
  6.8 2.3 %shard_map.29 = (bf16[768,2048]{1,0:T(8,128)(2,1)S(1)}, bf16[1024,1024]{1,0:T(8,128)(2,1)S(1)}) custom-call(f32[1,384]{1,0:T(1,128)S(1)} %get-tuple-element.12.kept_ref), custom_call_target="tpu_custom_call" | custom-call | flops 10000000 | bytes 20000000 | tf_op jit(solution)/shard_map/pallas_call | solution.py:214
  9.1 0.4 fusion.5.weights_ref
  9.5 2.0 %collective-permute-done.halo_ref = bf16[16,4,2048]{2,1,0:T(4,128)(2,1)S(1)} collective-permute-done((bf16[16,4,2048]{2,1,0:T(4,128)(2,1)S(1)}, bf16[16,4,2048]{2,1,0:T(4,128)(2,1)S(1)}, u32[]{:S(2)}, u32[]{:S(2)}) %collective-permute-start) | collective-permute-done | bytes 262176 | tf_op jit(solution)/shard_map/ppermute | solution.py:212
  11.5 0.0 copy-done.1
  11.5 4.2 %shard_map.30 = bf16[64,4,1152]{2,1,0:T(4,128)(2,1)S(1)} custom-call(bf16[768,2048]{1,0:T(8,128)(2,1)S(1)} %get-tuple-element.13.table_ref, bf16[16,24,2048]{2,1,0:T(8,128)(2,1)S(1)} %copy-done.1, bf16[16,4,2048]{2,1,0:T(4,128)(2,1)S(1)} %collective-permute-done.halo_ref, f32[4,2048]{1,0:T(4,128)S(1)} %fusion.5.weights_ref), custom_call_target="tpu_custom_call" | custom-call | tf_op jit(solution)/shard_map/pallas_call | solution.py:226
  15.7 51.7 %all_to_all.5.owned_ref = bf16[64,4,1152]{2,1,0:T(4,128)(2,1)S(1)} all-to-all(bf16[64,4,1152]{2,1,0:T(4,128)(2,1)S(1)} %shard_map.30), channel_id=1, replica_groups=mesh['inp'=64,'tblk'=8] {'inp'}, dimensions={0} | all-to-all | bytes 1179648 | tf_op jit(solution)/shard_map/all_to_all | solution.py:234
  67.3 1.5 %shard_map.31 = (bf16[288,1024]{1,0:T(8,128)(2,1)S(1)}, bf16[144,1024]{1,0:T(8,128)(2,1)S(1)}, bf16[144,1024]{1,0:T(8,128)(2,1)S(1)}) custom-call(bf16[64,4,1152]{2,1,0:T(4,128)(2,1)S(1)} %all_to_all.5.owned_ref, bf16[1024,1024]{1,0:T(8,128)(2,1)S(1)} %get-tuple-element.15.swap_ref), custom_call_target="tpu_custom_call" | custom-call | tf_op jit(solution)/shard_map/pallas_call | solution.py:236
  68.8 1.9 %collective-permute-start.3 = (bf16[144,1024]{1,0:T(8,128)(2,1)S(1)}, bf16[144,1024]{1,0:T(8,128)(2,1)S(1)}, u32[]{:S(2)}, u32[]{:S(2)}) collective-permute-start(bf16[144,1024]{1,0:T(8,128)(2,1)S(1)} %get-tuple-element.16), channel_id=1, source_target_pairs={{0,2},{1,3},{2,4},{3,5},{4,6},{5,7},{6,0},{7,1},{8,10},{9,11},{10,... | collective-permute-start | bytes 884744 | tf_op jit(solution)/shard_map/ppermute | solution.py:244
  70.7 4.6 %collective-permute-start.5 = (bf16[144,1024]{1,0:T(8,128)(2,1)S(1)}, bf16[144,1024]{1,0:T(8,128)(2,1)S(1)}, u32[]{:S(2)}, u32[]{:S(2)}) collective-permute-start(bf16[144,1024]{1,0:T(8,128)(2,1)S(1)} %get-tuple-element.17), channel_id=1, source_target_pairs={{0,6},{1,7},{2,0},{3,1},{4,2},{5,3},{6,4},{7,5},{8,14},{9,15},{10,... | collective-permute-start | bytes 884744 | tf_op jit(solution)/shard_map/ppermute | solution.py:244
  75.3 1.9 %collective-permute-start.1 = (bf16[144,1024]{1,0:T(8,128)(2,1)S(1)}, bf16[144,1024]{1,0:T(8,128)(2,1)S(1)}, u32[]{:S(2)}, u32[]{:S(2)}) collective-permute-start(bf16[144,1024]{1,0:T(8,128)(2,1)S(1)} %get-tuple-element.16), channel_id=1, source_target_pairs={{0,6},{1,7},{2,0},{3,1},{4,2},{5,3},{6,4},{7,5},{8,14},{9,15},{10,... | collective-permute-start | bytes 884744 | tf_op jit(solution)/shard_map/ppermute | solution.py:244
  77.2 3.4 %collective-permute-start.2 = (bf16[144,1024]{1,0:T(8,128)(2,1)S(1)}, bf16[144,1024]{1,0:T(8,128)(2,1)S(1)}, u32[]{:S(2)}, u32[]{:S(2)}) collective-permute-start(bf16[144,1024]{1,0:T(8,128)(2,1)S(1)} %get-tuple-element.17), channel_id=1, source_target_pairs={{0,2},{1,3},{2,4},{3,5},{4,6},{5,7},{6,0},{7,1},{8,10},{9,11},{10,... | collective-permute-start | bytes 884744 | tf_op jit(solution)/shard_map/ppermute | solution.py:244
  80.6 0.2 collective-permute-done.3.refs_1_
  80.8 1.9 %collective-permute-start.4 = (bf16[144,1024]{1,0:T(8,128)(2,1)S(1)}, bf16[144,1024]{1,0:T(8,128)(2,1)S(1)}, u32[]{:S(2)}, u32[]{:S(2)}) collective-permute-start(bf16[144,1024]{1,0:T(8,128)(2,1)S(1)} %collective-permute-done.3.refs_1_), channel_id=1, source_target_pairs={{0,2},{1,3},{2,4},{3,5},{4,6},{5,7},{6,0},{7,1},{8,10},{9,11},{10,... | collective-permute-start | bytes 884744 | tf_op jit(solution)/shard_map/ppermute | solution.py:244
  82.7 0.0 collective-permute-done.5.refs_2_
  82.7 4.6 %collective-permute-start.6 = (bf16[144,1024]{1,0:T(8,128)(2,1)S(1)}, bf16[144,1024]{1,0:T(8,128)(2,1)S(1)}, u32[]{:S(2)}, u32[]{:S(2)}) collective-permute-start(bf16[144,1024]{1,0:T(8,128)(2,1)S(1)} %collective-permute-done.5.refs_2_), channel_id=1, source_target_pairs={{0,6},{1,7},{2,0},{3,1},{4,2},{5,3},{6,4},{7,5},{8,14},{9,15},{10,... | collective-permute-start | bytes 884744 | tf_op jit(solution)/shard_map/ppermute | solution.py:244
  87.3 0.1 shard_map.33.near
  87.4 3.5 %collective-permute-start.8 = (bf16[576,1024]{1,0:T(8,128)(2,1)S(1)}, bf16[576,1024]{1,0:T(8,128)(2,1)S(1)}, u32[]{:S(2)}, u32[]{:S(2)}) collective-permute-start(bf16[576,1024]{1,0:T(8,128)(2,1)S(1)} %shard_map.33.near), channel_id=1, source_target_pairs={{0,1},{1,0},{2,3},{3,2},{4,5},{5,4},{6,7},{7,6},{8,9},{9,8},{10,11... | collective-permute-start | bytes 3538952 | tf_op jit(solution)/shard_map/ppermute | solution.py:245
  90.9 0.0 collective-permute-done.1.refs_0_
  90.9 0.0 collective-permute-done.2.refs_1_
  90.9 1.9 %collective-permute-done.4.refs_2_ = bf16[144,1024]{1,0:T(8,128)(2,1)S(1)} collective-permute-done((bf16[144,1024]{1,0:T(8,128)(2,1)S(1)}, bf16[144,1024]{1,0:T(8,128)(2,1)S(1)}, u32[]{:S(2)}, u32[]{:S(2)}) %collective-permute-start.4) | collective-permute-done | bytes 294944 | tf_op jit(solution)/shard_map/ppermute | solution.py:244
  92.8 0.7 collective-permute-done.6.refs_3_
  93.6 0.1 shard_map.32.rest
  93.7 4.4 %collective-permute-start.7 = (bf16[576,1024]{1,0:T(8,128)(2,1)S(1)}, bf16[576,1024]{1,0:T(8,128)(2,1)}, u32[]{:S(2)}, u32[]{:S(2)}) collective-permute-start(bf16[576,1024]{1,0:T(8,128)(2,1)S(1)} %shard_map.32.rest), channel_id=1, source_target_pairs={{0,1},{1,0},{2,3},{3,2},{4,5},{5,4},{6,7},{7,6},{8,9},{9,8},{10,11... | collective-permute-start | bytes 3538952 | tf_op jit(solution)/shard_map/ppermute | solution.py:245
  98.1 0.0 collective-permute-done.8.near_o
  98.1 1.8 %shard_map.34.part_ref = f32[6,256,1024]{2,1,0:T(8,128)S(1)} custom-call(s32[1]{0:T(128)} %bitcast.block_ref, bf16[576,1024]{1,0:T(8,128)(2,1)S(1)} %shard_map.33.near, bf16[576,1024]{1,0:T(8,128)(2,1)S(1)} %shard_map.32.rest, bf16[576,1024]{1,0:T(8,128)(2,1)S(1)} %collective-permute-done.8.near_o), custom_call_target="tpu_custom_call" | custom-call | flops 600000000 | bytes 9000000 | tf_op jit(solution)/shard_map/pallas_call | solution.py:263
  99.9 0.7 collective-permute-done.7
  100.7 3.4 %shard_map.35 = bf16[6,2,128,1024]{3,2,1,0:T(8,128)(2,1)} custom-call(s32[1]{0:T(128)} %bitcast.block_ref, bf16[2,288,1024]{2,1,0:T(8,128)(2,1)} %bitcast.1.rest_o, f32[6,256,1024]{2,1,0:T(8,128)S(1)} %shard_map.34.part_ref), custom_call_target="tpu_custom_call" | custom-call | tf_op jit(solution)/shard_map/pallas_call | solution.py:271
  (1 shorter events, 0.0 us)
Async XLA Ops:
  0.0 1.4 %copy-start = (bf16[16,24,2048]{2,1,0:T(8,128)(2,1)S(1)}, bf16[16,24,2048]{2,1,0:T(8,128)(2,1)}, u32[]{:S(2)}) copy-start(bf16[16,24,2048]{2,1,0:T(8,128)(2,1)} %samples_ref.3) | copy-start | bytes 4718596
  1.4 0.7 copy-start.2
  2.1 9.4 %copy-start.1 = (bf16[16,24,2048]{2,1,0:T(8,128)(2,1)S(1)}, bf16[16,24,2048]{2,1,0:T(8,128)(2,1)}, u32[]{:S(2)}) copy-start(bf16[16,24,2048]{2,1,0:T(8,128)(2,1)} %samples_ref.3) | copy-start | bytes 4718596
  2.1 9.3 %collective-permute-start = (bf16[16,4,2048]{2,1,0:T(4,128)(2,1)S(1)}, bf16[16,4,2048]{2,1,0:T(4,128)(2,1)S(1)}, u32[]{:S(2)}, u32[]{:S(2)}) collective-permute-start(bf16[16,4,2048]{2,1,0:T(4,128)(2,1)S(1)} %get-tuple-element.14), channel_id=1, source_target_pairs={{0,1},{1,2},{2,3},{3,4},{4,5},{5,6},{6,7},{8,9},{9,10},{10,11},{11... | collective-permute-start | bytes 786440 | tf_op jit(solution)/shard_map/ppermute | solution.py:212
  68.8 12.0 %collective-permute-start.3 = (bf16[144,1024]{1,0:T(8,128)(2,1)S(1)}, bf16[144,1024]{1,0:T(8,128)(2,1)S(1)}, u32[]{:S(2)}, u32[]{:S(2)}) collective-permute-start(bf16[144,1024]{1,0:T(8,128)(2,1)S(1)} %get-tuple-element.16), channel_id=1, source_target_pairs={{0,2},{1,3},{2,4},{3,5},{4,6},{5,7},{6,0},{7,1},{8,10},{9,11},{10,... | collective-permute-start | bytes 884744 | tf_op jit(solution)/shard_map/ppermute | solution.py:244
  70.7 12.0 %collective-permute-start.5 = (bf16[144,1024]{1,0:T(8,128)(2,1)S(1)}, bf16[144,1024]{1,0:T(8,128)(2,1)S(1)}, u32[]{:S(2)}, u32[]{:S(2)}) collective-permute-start(bf16[144,1024]{1,0:T(8,128)(2,1)S(1)} %get-tuple-element.17), channel_id=1, source_target_pairs={{0,6},{1,7},{2,0},{3,1},{4,2},{5,3},{6,4},{7,5},{8,14},{9,15},{10,... | collective-permute-start | bytes 884744 | tf_op jit(solution)/shard_map/ppermute | solution.py:244
  75.3 15.6 %collective-permute-start.1 = (bf16[144,1024]{1,0:T(8,128)(2,1)S(1)}, bf16[144,1024]{1,0:T(8,128)(2,1)S(1)}, u32[]{:S(2)}, u32[]{:S(2)}) collective-permute-start(bf16[144,1024]{1,0:T(8,128)(2,1)S(1)} %get-tuple-element.16), channel_id=1, source_target_pairs={{0,6},{1,7},{2,0},{3,1},{4,2},{5,3},{6,4},{7,5},{8,14},{9,15},{10,... | collective-permute-start | bytes 884744 | tf_op jit(solution)/shard_map/ppermute | solution.py:244
  77.2 13.7 %collective-permute-start.2 = (bf16[144,1024]{1,0:T(8,128)(2,1)S(1)}, bf16[144,1024]{1,0:T(8,128)(2,1)S(1)}, u32[]{:S(2)}, u32[]{:S(2)}) collective-permute-start(bf16[144,1024]{1,0:T(8,128)(2,1)S(1)} %get-tuple-element.17), channel_id=1, source_target_pairs={{0,2},{1,3},{2,4},{3,5},{4,6},{5,7},{6,0},{7,1},{8,10},{9,11},{10,... | collective-permute-start | bytes 884744 | tf_op jit(solution)/shard_map/ppermute | solution.py:244
  80.8 12.1 %collective-permute-start.4 = (bf16[144,1024]{1,0:T(8,128)(2,1)S(1)}, bf16[144,1024]{1,0:T(8,128)(2,1)S(1)}, u32[]{:S(2)}, u32[]{:S(2)}) collective-permute-start(bf16[144,1024]{1,0:T(8,128)(2,1)S(1)} %collective-permute-done.3.refs_1_), channel_id=1, source_target_pairs={{0,2},{1,3},{2,4},{3,5},{4,6},{5,7},{6,0},{7,1},{8,10},{9,11},{10,... | collective-permute-start | bytes 884744 | tf_op jit(solution)/shard_map/ppermute | solution.py:244
  82.7 10.9 %collective-permute-start.6 = (bf16[144,1024]{1,0:T(8,128)(2,1)S(1)}, bf16[144,1024]{1,0:T(8,128)(2,1)S(1)}, u32[]{:S(2)}, u32[]{:S(2)}) collective-permute-start(bf16[144,1024]{1,0:T(8,128)(2,1)S(1)} %collective-permute-done.5.refs_2_), channel_id=1, source_target_pairs={{0,6},{1,7},{2,0},{3,1},{4,2},{5,3},{6,4},{7,5},{8,14},{9,15},{10,... | collective-permute-start | bytes 884744 | tf_op jit(solution)/shard_map/ppermute | solution.py:244
  87.4 10.7 %collective-permute-start.8 = (bf16[576,1024]{1,0:T(8,128)(2,1)S(1)}, bf16[576,1024]{1,0:T(8,128)(2,1)S(1)}, u32[]{:S(2)}, u32[]{:S(2)}) collective-permute-start(bf16[576,1024]{1,0:T(8,128)(2,1)S(1)} %shard_map.33.near), channel_id=1, source_target_pairs={{0,1},{1,0},{2,3},{3,2},{4,5},{5,4},{6,7},{7,6},{8,9},{9,8},{10,11... | collective-permute-start | bytes 3538952 | tf_op jit(solution)/shard_map/ppermute | solution.py:245
  93.7 7.0 %collective-permute-start.7 = (bf16[576,1024]{1,0:T(8,128)(2,1)S(1)}, bf16[576,1024]{1,0:T(8,128)(2,1)}, u32[]{:S(2)}, u32[]{:S(2)}) collective-permute-start(bf16[576,1024]{1,0:T(8,128)(2,1)S(1)} %shard_map.32.rest), channel_id=1, source_target_pairs={{0,1},{1,0},{2,3},{3,2},{4,5},{5,4},{6,7},{7,6},{8,9},{9,8},{10,11... | collective-permute-start | bytes 3538952 | tf_op jit(solution)/shard_map/ppermute | solution.py:245
